TPU v7x, 32 devices: a whole 2x2x4 slice. The times are simulated.
32 devices in a mesh: grp: 2 (over x), inp: 4 (over y, core), tm: 4 (over z).
Axes of the slice: x: 2, y: 2, z: 4, core: 2. Of those that a mesh axis runs over, the one named last changes fastest.
Arguments:
- samples: bfloat16 [64, 1024, 8192], P(('grp', 'tm'), 'inp'), parts along dimension 0, may hold values from -6 to 6
- fir: float32 [16, 8192], replicated, may hold values from -1 to 1
- flags: int32 [64, 1024], P(('grp', 'tm'), 'inp'), parts along dimension 0, may hold values 0 or 1
Outputs:
- visibilities: float32 [16, 2, 1024, 1024], P(('grp', 'tm'), None, 'inp'), parts along dimension 0
There are 2 independent parts, one for each index of `grp`. A program takes and returns all parts, laid end to end along the dimension named above; an argument that names none is the same for every part. Nothing has to cross between parts.
All inputs are finite; a program needn't handle non-finite values. No bound on the sum of `flags` on one device may be relied on, other than what follows from the above.
Results may differ from a plain program's by a relative error of at most 0.0063.
Values may be sent and summed in bfloat16 or wider, within the bound.
No kernel may reach another device: no remote copies, remote signals or barrier semaphores. Data moves between devices by JAX's collectives and lax.ppermute only.
A program may use at most 256 MiB of HBM per device.

v0:
```python
import functools

import jax
import jax.numpy as jnp
import ml_dtypes
import numpy as np
from jax import lax
from jax.experimental import pallas as pl
from jax.experimental.pallas import tpu as pltpu
from jax.sharding import PartitionSpec as P

NCH = 4096
CH_DEV = 2
SUBLANES = 8
LANES = 128
ROW_TILE = 16
FLAGGED = 1e30
MIB = 1 << 20


def round_up(value, step):
    return -(-value // step) * step


def partner(index, distance, count):
    if count & (count - 1) == 0:
        return index ^ distance
    return (distance - index) % count


def exchange(value, axis, distance):
    count = lax.axis_size(axis)
    return lax.ppermute(value, axis, [(source, partner(source, distance, count)) for source in range(count)])


def slab_table(length, slabs, lowest):
    sample_ids = np.arange(length, dtype=np.int64)
    channel_ids = lowest + np.arange(slabs * CH_DEV, dtype=np.int64)
    angle = 2.0 * np.pi / length * (channel_ids[:, None] * sample_ids[None, :] % length)
    factor = np.sqrt(2.0 / length)
    both = np.stack([factor * np.cos(angle), -factor * np.sin(angle)], axis=0)
    by_slab = both.reshape(2, slabs, CH_DEV, length).transpose(1, 0, 2, 3).reshape(slabs, 2 * CH_DEV, length)
    return np.tile(by_slab, (1, SUBLANES // (2 * CH_DEV), 1)).astype(ml_dtypes.bfloat16)


def channelize(slabs, window, me_ref, samples_ref, fir_ref, table_ref, flags_ref, *rest):
    outs, (weights, sums, total) = rest[:slabs], rest[slabs:]
    step = pl.program_id(0)
    frames, inputs, width = samples_ref.shape
    taps = fir_ref.shape[0]
    group = 2 * CH_DEV
    per_slab = taps * group
    pack = SUBLANES // group
    row_ids = lax.broadcasted_iota(jnp.int32, (SUBLANES, width), 0)

    @pl.when(step == 0)
    def _():
        sums[...] = jnp.zeros_like(sums)

    tables = [table_ref[partner(me_ref[0], slot, slabs)].astype(jnp.float32) for slot in range(slabs)]
    for first in range(0, taps, 2 * pack):
        coefs = []
        for half in range(2):
            coef = None
            for place in range(pack):
                tap = taps - 1 - (first + half * pack + place)
                line = jnp.broadcast_to(fir_ref[tap : tap + 1, :], (SUBLANES, width))
                coef = line if coef is None else jnp.where(row_ids >= place * group, line, coef)
            coefs.append(coef)
        for slot in range(slabs):
            rows = jnp.concatenate([coef * tables[slot] for coef in coefs], axis=0)
            weights[pl.ds(slot * per_slab + first * group, ROW_TILE), :] = rows.astype(jnp.bfloat16)

    for frame in range(frames):
        sums[frame] += lax.dot_general(
            weights[...], samples_ref[frame], (((1,), (1,)), ((), ())), preferred_element_type=jnp.float32
        )

    @pl.when(step == pl.num_programs(0) - 1)
    def _():
        for slot in range(slabs):
            total[...] = jnp.zeros_like(total)
            for frame in range(frames):
                total[pl.ds(frame * group, per_slab), :] += sums[frame, pl.ds(slot * per_slab, per_slab), :]
            good = jnp.broadcast_to(flags_ref[...][:, None, :], (frames, group, inputs)).reshape(frames * group, inputs)
            own = frames * group
            total[0:own, :] = jnp.where(good == 0, FLAGGED, total[0:own, :])
            outs[slot][...] = total[...].astype(outs[slot].dtype)


def add_hops(slabs, frames, me_ref, *rest):
    pieces, (out_ref, total) = rest[:slabs], rest[slabs:]
    group = 2 * CH_DEV
    total[...] = jnp.zeros_like(total)
    for slot in range(slabs):
        place = pl.multiple_of(partner(me_ref[0], slot, slabs) * (frames * group), SUBLANES)
        total[pl.ds(place, pieces[slot].shape[0]), :] += pieces[slot][...].astype(jnp.float32)
    value = total[0 : out_ref.shape[0], :]
    out_ref[...] = jnp.where(value > 0.5 * FLAGGED, 0.0, value).astype(out_ref.dtype)


def correlate(scale, me_ref, own_ref, *rest):
    pieces, (out_ref, left) = rest[:-2], rest[-2:]
    step = pl.program_id(0)
    rows, inputs = own_ref.shape
    group = 2 * CH_DEV

    @pl.when(step == 0)
    def _():
        own = own_ref[...].astype(jnp.float32)
        row_ids = lax.broadcasted_iota(jnp.int32, own.shape, 0)
        is_real = row_ids % group < CH_DEV
        turned = jnp.where(is_real, pltpu.roll(own, rows - CH_DEV, 0), -pltpu.roll(own, CH_DEV, 0))
        for channel in range(CH_DEV):
            keep = row_ids % CH_DEV == channel
            for part, value in enumerate((own, turned)):
                place = (channel * 2 + part) * inputs
                left[pl.ds(place, inputs), :] = jnp.where(keep, value, 0.0).T.astype(left.dtype)

    for slot, piece in enumerate(pieces):
        @pl.when(step == slot)
        def _(piece=piece):
            product = jnp.dot(left[...], piece[...], preferred_element_type=jnp.float32)
            out_ref[...] = (product * scale).reshape(out_ref.shape)


def shards(samples, fir, flags):
    frames, inputs, length = samples.shape
    taps = fir.shape[0]
    slabs = lax.axis_size("tm")
    blocks = lax.axis_size("inp")
    group = 2 * CH_DEV
    window = frames + taps - 1
    rows = round_up(window * group, ROW_TILE)
    spectra_rows = slabs * frames * group
    width = min(length, 1024)
    table = jnp.asarray(slab_table(length, slabs, NCH // 4))
    my_slab = lax.axis_index("tm").astype(jnp.int32).reshape(1)
    my_block = lax.axis_index("inp").astype(jnp.int32).reshape(1)

    sent = pl.pallas_call(
        functools.partial(channelize, slabs, window),
        grid_spec=pltpu.PrefetchScalarGridSpec(
            num_scalar_prefetch=1,
            grid=(length // width,),
            in_specs=[
                pl.BlockSpec((frames, inputs, width), lambda step, me: (0, 0, step)),
                pl.BlockSpec((taps, width), lambda step, me: (0, step)),
                pl.BlockSpec((slabs, SUBLANES, width), lambda step, me: (0, 0, step)),
                pl.BlockSpec((frames, inputs), lambda step, me: (0, 0)),
            ],
            out_specs=[pl.BlockSpec((rows, inputs), lambda step, me: (0, 0))] * slabs,
            scratch_shapes=[
                pltpu.VMEM((slabs * taps * group, width), jnp.bfloat16),
                pltpu.VMEM((frames, slabs * taps * group, inputs), jnp.float32),
                pltpu.VMEM((rows, inputs), jnp.float32),
            ],
        ),
        out_shape=[
            jax.ShapeDtypeStruct((rows, inputs), jnp.bfloat16 if slot else jnp.float32) for slot in range(slabs)
        ],
        compiler_params=pltpu.CompilerParams(vmem_limit_bytes=32 * MIB),
        name="channelize",
    )(my_slab, samples, fir, table, flags)

    pieces = [sent[0]] + [exchange(sent[slot], "tm", slot) for slot in range(1, slabs)]
    spectra = pl.pallas_call(
        functools.partial(add_hops, slabs, frames),
        grid_spec=pltpu.PrefetchScalarGridSpec(
            num_scalar_prefetch=1,
            grid=(1,),
            in_specs=[pl.BlockSpec((rows, inputs), lambda step, me: (0, 0))] * slabs,
            out_specs=pl.BlockSpec((spectra_rows, inputs), lambda step, me: (0, 0)),
            scratch_shapes=[pltpu.VMEM((spectra_rows + rows, inputs), jnp.float32)],
        ),
        out_shape=jax.ShapeDtypeStruct((spectra_rows, inputs), jnp.bfloat16),
        name="add_hops",
    )(my_slab, *pieces)

    if inputs % LANES == 0:
        gathered = [spectra] + [exchange(spectra, "inp", slot) for slot in range(1, blocks)]
    else:
        gathered = [lax.all_gather(spectra, "inp", axis=1, tiled=True)]
    columns = gathered[0].shape[1]
    return pl.pallas_call(
        functools.partial(correlate, 1.0 / (slabs * frames)),
        grid_spec=pltpu.PrefetchScalarGridSpec(
            num_scalar_prefetch=1,
            grid=(len(gathered),),
            in_specs=[pl.BlockSpec((spectra_rows, inputs), lambda step, me: (0, 0))]
            + [pl.BlockSpec((spectra_rows, columns), lambda step, me: (0, 0))] * len(gathered),
            out_specs=pl.BlockSpec(
                (CH_DEV, 2, inputs, columns),
                lambda step, me: (0, 0, 0, partner(me[0], step, blocks) if len(gathered) > 1 else 0),
            ),
            scratch_shapes=[pltpu.VMEM((CH_DEV * 2 * inputs, spectra_rows), jnp.bfloat16)],
        ),
        out_shape=jax.ShapeDtypeStruct((CH_DEV, 2, inputs, blocks * inputs), jnp.float32),
        name="correlate",
    )(my_block, spectra, *gathered)


def solution(mesh):
    in_specs = (P(("grp", "tm"), "inp", None), P(), P(("grp", "tm"), "inp"))
    out_specs = P(("grp", "tm"), None, "inp", None)
    return jax.shard_map(shards, mesh=mesh, in_specs=in_specs, out_specs=out_specs, check_vma=False)
```

profile of v0, /device:TPU:0, one launch (start us, length us, event | category | flops | bytes accessed | tf_op | source)
XLA Modules:
  0.0 43.9 jit_solution(3134865425011137105)
XLA Ops:
  0.0 1.0 %copy-done = f32[16,8192]{1,0:T(8,128)S(1)} copy-done((f32[16,8192]{1,0:T(8,128)S(1)}, f32[16,8192]{1,0:T(8,128)}, u32[]{:S(2)}) %copy-start) | copy-done | bytes 524312
  1.0 1.0 %copy-done.1 = bf16[4,8,8192]{2,1,0:T(8,128)(2,1)S(1)} copy-done((bf16[4,8,8192]{2,1,0:T(8,128)(2,1)S(1)}, bf16[4,8,8192]{2,1,0:T(8,128)(2,1)}, u32[]{:S(2)}) %copy-start.1) | copy-done | bytes 524312
  2.1 0.7 %copy-done.3 = s32[8,256]{1,0:T(8,128)S(1)} copy-done((s32[8,256]{1,0:T(8,128)S(1)}, s32[8,256]{1,0:T(8,128)}, u32[]{:S(2)}) %copy-start.3) | copy-done | bytes 8216
  2.8 16.1 %channelize.1 = (f32[96,256]{1,0:T(8,128)S(1)}, bf16[96,256]{1,0:T(8,128)(2,1)S(1)}, bf16[96,256]{1,0:T(8,128)(2,1)S(1)}, bf16[96,256]{1,0:T(8,128)(2,1)S(1)}) custom-call(s32[1]{0:T(128)} %bitcast.1.me_ref, bf16[8,256,8192]{2,1,0:T(8,128)(2,1)} %samples_ref.1, f32[16,8192]{1,0:T(8,128)S(1)} %copy-done, bf16[4,8,8192]{2,1,0:T(8,128)(2,1)S(1)} %copy-done.1, ...), custom_call_target="tpu_custom_call" | custom-call | tf_op jit(solution)/shard_map/channelize/pallas_call | solution.py:141
  18.9 0.0 copy-start.2
  18.9 0.6 %copy-done.2 = f32[96,256]{1,0:T(8,128)} copy-done((f32[96,256]{1,0:T(8,128)}, f32[96,256]{1,0:T(8,128)S(1)}, u32[]{:S(2)}) %copy-start.2) | copy-done | bytes 98328
  19.6 3.0 %collective-permute-start = (bf16[96,256]{1,0:T(8,128)(2,1)S(1)}, bf16[96,256]{1,0:T(8,128)(2,1)S(1)}, u32[]{:S(2)}, u32[]{:S(2)}) collective-permute-start(bf16[96,256]{1,0:T(8,128)(2,1)S(1)} %get-tuple-element.10), channel_id=1, source_target_pairs={{0,1},{1,0},{2,3},{3,2},{4,5},{5,4},{6,7},{7,6},{8,9},{9,8},{10,11... | collective-permute-start | bytes 147464 | tf_op jit(solution)/shard_map/ppermute | solution.py:33
  22.6 2.6 %collective-permute-start.1 = (bf16[96,256]{1,0:T(8,128)(2,1)S(1)}, bf16[96,256]{1,0:T(8,128)(2,1)S(1)}, u32[]{:S(2)}, u32[]{:S(2)}) collective-permute-start(bf16[96,256]{1,0:T(8,128)(2,1)S(1)} %get-tuple-element.11), channel_id=1, source_target_pairs={{0,2},{1,3},{2,0},{3,1},{4,6},{5,7},{6,4},{7,5},{8,10},{9,11},{10,... | collective-permute-start | bytes 147464 | tf_op jit(solution)/shard_map/ppermute | solution.py:33
  25.2 0.0 collective-permute-start.2
  25.2 0.0 collective-permute-done.rest_1_
  25.2 3.3 %collective-permute-done.1.rest_2_ = bf16[96,256]{1,0:T(8,128)(2,1)S(1)} collective-permute-done((bf16[96,256]{1,0:T(8,128)(2,1)S(1)}, bf16[96,256]{1,0:T(8,128)(2,1)S(1)}, u32[]{:S(2)}, u32[]{:S(2)}) %collective-permute-start.1) | collective-permute-done | bytes 49184 | tf_op jit(solution)/shard_map/ppermute | solution.py:33
  28.5 2.6 %collective-permute-done.2.rest_3_ = bf16[96,256]{1,0:T(8,128)(2,1)S(1)} collective-permute-done((bf16[96,256]{1,0:T(8,128)(2,1)S(1)}, bf16[96,256]{1,0:T(8,128)(2,1)S(1)}, u32[]{:S(2)}, u32[]{:S(2)}) %collective-permute-start.2) | collective-permute-done | bytes 49184 | tf_op jit(solution)/shard_map/ppermute | solution.py:33
  31.1 0.0 copy-done.7
  31.1 0.6 %copy-done.9 = bf16[96,256]{1,0:T(8,128)(2,1)} copy-done((bf16[96,256]{1,0:T(8,128)(2,1)}, bf16[96,256]{1,0:T(8,128)(2,1)S(1)}, u32[]{:S(2)}) %copy-start.9) | copy-done | bytes 49176
  31.7 1.6 %add_hops.1.own_ref.rest_0_ = bf16[128,256]{1,0:T(8,128)(2,1)} custom-call(s32[1]{0:T(128)} %bitcast.1.me_ref, f32[96,256]{1,0:T(8,128)} %copy-done.2, bf16[96,256]{1,0:T(8,128)(2,1)} %copy-done.7, bf16[96,256]{1,0:T(8,128)(2,1)} %copy-done.8, bf16[96,256]{1,0:T(8,128)(2,1)} %copy-done.9), custom_call_target="tpu_custom_call" | custom-call | tf_op jit(solution)/shard_map/add_hops/pallas_call | solution.py:167
  33.3 0.0 collective-permute-start.5
  33.3 1.5 %collective-permute-start.4 = (bf16[128,256]{1,0:T(8,128)(2,1)}, bf16[128,256]{1,0:T(8,128)(2,1)S(1)}, u32[]{:S(2)}, u32[]{:S(2)}) collective-permute-start(bf16[128,256]{1,0:T(8,128)(2,1)} %add_hops.1.own_ref.rest_0_), channel_id=1, source_target_pairs={{0,8},{4,12},{8,0},{12,4},{1,9},{5,13},{9,1},{13,5},{2,10},{6,14},... | collective-permute-start | bytes 196616 | tf_op jit(solution)/shard_map/ppermute | solution.py:33
  34.9 0.3 collective-permute-start.3
  35.2 2.7 %collective-permute-done.5.rest_3_ = bf16[128,256]{1,0:T(8,128)(2,1)S(1)} collective-permute-done((bf16[128,256]{1,0:T(8,128)(2,1)}, bf16[128,256]{1,0:T(8,128)(2,1)S(1)}, u32[]{:S(2)}, u32[]{:S(2)}) %collective-permute-start.5) | collective-permute-done | bytes 65568 | tf_op jit(solution)/shard_map/ppermute | solution.py:33
  37.9 1.5 %collective-permute-done.4.rest_2_ = bf16[128,256]{1,0:T(8,128)(2,1)S(1)} collective-permute-done((bf16[128,256]{1,0:T(8,128)(2,1)}, bf16[128,256]{1,0:T(8,128)(2,1)S(1)}, u32[]{:S(2)}, u32[]{:S(2)}) %collective-permute-start.4) | collective-permute-done | bytes 65568 | tf_op jit(solution)/shard_map/ppermute | solution.py:33
  39.3 0.0 collective-permute-done.3.rest_1_
  39.3 0.6 %copy-done.5 = bf16[128,256]{1,0:T(8,128)(2,1)} copy-done((bf16[128,256]{1,0:T(8,128)(2,1)}, bf16[128,256]{1,0:T(8,128)(2,1)S(1)}, u32[]{:S(2)}) %copy-start.5) | copy-done | bytes 65560
  39.9 0.0 copy-done.6
  40.0 3.9 %correlate.1 = f32[2,2,256,1024]{3,2,1,0:T(8,128)} custom-call(s32[1]{0:T(128)} %bitcast.me_ref, bf16[128,256]{1,0:T(8,128)(2,1)} %add_hops.1.own_ref.rest_0_, bf16[128,256]{1,0:T(8,128)(2,1)} %add_hops.1.own_ref.rest_0_, bf16[128,256]{1,0:T(8,128)(2,1)} %copy-done.6, bf16[128,256]{1,0:T(8,128)(2,1)} %copy-done.5, bf16[128,256]{1,0:T(8,128)(2,1)} %copy-done.4), custom_call_target="tpu_custom_call" | custom-call | tf_op jit(solution)/shard_map/correlate/pallas_call | solution.py:185
  (11 shorter events, 0.0 us)
Async XLA Ops:
  0.0 1.0 %copy-start = (f32[16,8192]{1,0:T(8,128)S(1)}, f32[16,8192]{1,0:T(8,128)}, u32[]{:S(2)}) copy-start(f32[16,8192]{1,0:T(8,128)} %fir_ref.1) | copy-start | bytes 1572868
  1.0 1.0 %copy-start.1 = (bf16[4,8,8192]{2,1,0:T(8,128)(2,1)S(1)}, bf16[4,8,8192]{2,1,0:T(8,128)(2,1)}, u32[]{:S(2)}) copy-start(bf16[4,8,8192]{2,1,0:T(8,128)(2,1)} %constant.9.clone.table_ref) | copy-start | bytes 1572868
  2.1 0.7 %copy-start.3 = (s32[8,256]{1,0:T(8,128)S(1)}, s32[8,256]{1,0:T(8,128)}, u32[]{:S(2)}) copy-start(s32[8,256]{1,0:T(8,128)} %flags_ref.1) | copy-start | bytes 24580
  18.9 0.6 %copy-start.2 = (f32[96,256]{1,0:T(8,128)}, f32[96,256]{1,0:T(8,128)S(1)}, u32[]{:S(2)}) copy-start(f32[96,256]{1,0:T(8,128)S(1)} %get-tuple-element.9.rest_0_) | copy-start | bytes 294916
  19.6 5.6 %collective-permute-start = (bf16[96,256]{1,0:T(8,128)(2,1)S(1)}, bf16[96,256]{1,0:T(8,128)(2,1)S(1)}, u32[]{:S(2)}, u32[]{:S(2)}) collective-permute-start(bf16[96,256]{1,0:T(8,128)(2,1)S(1)} %get-tuple-element.10), channel_id=1, source_target_pairs={{0,1},{1,0},{2,3},{3,2},{4,5},{5,4},{6,7},{7,6},{8,9},{9,8},{10,11... | collective-permute-start | bytes 147464 | tf_op jit(solution)/shard_map/ppermute | solution.py:33
  22.6 5.9 %collective-permute-start.1 = (bf16[96,256]{1,0:T(8,128)(2,1)S(1)}, bf16[96,256]{1,0:T(8,128)(2,1)S(1)}, u32[]{:S(2)}, u32[]{:S(2)}) collective-permute-start(bf16[96,256]{1,0:T(8,128)(2,1)S(1)} %get-tuple-element.11), channel_id=1, source_target_pairs={{0,2},{1,3},{2,0},{3,1},{4,6},{5,7},{6,4},{7,5},{8,10},{9,11},{10,... | collective-permute-start | bytes 147464 | tf_op jit(solution)/shard_map/ppermute | solution.py:33
  25.2 5.9 %collective-permute-start.2 = (bf16[96,256]{1,0:T(8,128)(2,1)S(1)}, bf16[96,256]{1,0:T(8,128)(2,1)S(1)}, u32[]{:S(2)}, u32[]{:S(2)}) collective-permute-start(bf16[96,256]{1,0:T(8,128)(2,1)S(1)} %get-tuple-element.12), channel_id=1, source_target_pairs={{0,3},{1,2},{2,1},{3,0},{4,7},{5,6},{6,5},{7,4},{8,11},{9,10},{10,... | collective-permute-start | bytes 147464 | tf_op jit(solution)/shard_map/ppermute | solution.py:33
  25.2 5.9 %copy-start.7 = (bf16[96,256]{1,0:T(8,128)(2,1)}, bf16[96,256]{1,0:T(8,128)(2,1)S(1)}, u32[]{:S(2)}) copy-start(bf16[96,256]{1,0:T(8,128)(2,1)S(1)} %collective-permute-done.rest_1_) | copy-start | bytes 147460
  28.5 2.6 %copy-start.8 = (bf16[96,256]{1,0:T(8,128)(2,1)}, bf16[96,256]{1,0:T(8,128)(2,1)S(1)}, u32[]{:S(2)}) copy-start(bf16[96,256]{1,0:T(8,128)(2,1)S(1)} %collective-permute-done.1.rest_2_) | copy-start | bytes 147460
  31.1 0.6 %copy-start.9 = (bf16[96,256]{1,0:T(8,128)(2,1)}, bf16[96,256]{1,0:T(8,128)(2,1)S(1)}, u32[]{:S(2)}) copy-start(bf16[96,256]{1,0:T(8,128)(2,1)S(1)} %collective-permute-done.2.rest_3_) | copy-start | bytes 147460
  33.3 4.5 %collective-permute-start.5 = (bf16[128,256]{1,0:T(8,128)(2,1)}, bf16[128,256]{1,0:T(8,128)(2,1)S(1)}, u32[]{:S(2)}, u32[]{:S(2)}) collective-permute-start(bf16[128,256]{1,0:T(8,128)(2,1)} %add_hops.1.own_ref.rest_0_), channel_id=1, source_target_pairs={{0,12},{4,8},{8,4},{12,0},{1,13},{5,9},{9,5},{13,1},{2,14},{6,10},... | collective-permute-start | bytes 196616 | tf_op jit(solution)/shard_map/ppermute | solution.py:33
  33.3 6.0 %collective-permute-start.4 = (bf16[128,256]{1,0:T(8,128)(2,1)}, bf16[128,256]{1,0:T(8,128)(2,1)S(1)}, u32[]{:S(2)}, u32[]{:S(2)}) collective-permute-start(bf16[128,256]{1,0:T(8,128)(2,1)} %add_hops.1.own_ref.rest_0_), channel_id=1, source_target_pairs={{0,8},{4,12},{8,0},{12,4},{1,9},{5,13},{9,1},{13,5},{2,10},{6,14},... | collective-permute-start | bytes 196616 | tf_op jit(solution)/shard_map/ppermute | solution.py:33
  34.9 4.5 %collective-permute-start.3 = (bf16[128,256]{1,0:T(8,128)(2,1)}, bf16[128,256]{1,0:T(8,128)(2,1)S(1)}, u32[]{:S(2)}, u32[]{:S(2)}) collective-permute-start(bf16[128,256]{1,0:T(8,128)(2,1)} %add_hops.1.own_ref.rest_0_), channel_id=1, source_target_pairs={{0,4},{4,0},{8,12},{12,8},{1,5},{5,1},{9,13},{13,9},{2,6},{6,2},{1... | collective-permute-start | bytes 196616 | tf_op jit(solution)/shard_map/ppermute | solution.py:33
  37.8 1.5 %copy-start.4 = (bf16[128,256]{1,0:T(8,128)(2,1)}, bf16[128,256]{1,0:T(8,128)(2,1)S(1)}, u32[]{:S(2)}) copy-start(bf16[128,256]{1,0:T(8,128)(2,1)S(1)} %collective-permute-done.5.rest_3_) | copy-start | bytes 196612
  39.3 0.6 %copy-start.5 = (bf16[128,256]{1,0:T(8,128)(2,1)}, bf16[128,256]{1,0:T(8,128)(2,1)S(1)}, u32[]{:S(2)}) copy-start(bf16[128,256]{1,0:T(8,128)(2,1)S(1)} %collective-permute-done.4.rest_2_) | copy-start | bytes 196612
  39.3 0.6 %copy-start.6 = (bf16[128,256]{1,0:T(8,128)(2,1)}, bf16[128,256]{1,0:T(8,128)(2,1)S(1)}, u32[]{:S(2)}) copy-start(bf16[128,256]{1,0:T(8,128)(2,1)S(1)} %collective-permute-done.3.rest_1_) | copy-start | bytes 196612
where the time goes:
time: 44.4 us; the launch traced here: 43.9 us
  Pallas kernels  21.7 us (49%)
  waiting for transfers between devices  10 us (23%)
  starting transfers between devices  7.48 us (17%)
  local copies, waits for them, and re-layouts  4.66 us (10%)
    pallas_call x1, Pallas kernels, shards(): pl.pallas_call(functools.partial(channelize, slabs, window), grid_spec=pl...  16.1 us
    ppermute x6, waiting for transfers between devices, exchange(): lax.ppermute(value, axis, [(source, partner(source, distance, count)) for...  10 us
    ppermute x6, starting transfers between devices, exchange(): lax.ppermute(value, axis, [(source, partner(source, distance, count)) for...  7.48 us
    unnamed x20, local copies, waits for them, and re-layouts  4.66 us
    pallas_call x1, Pallas kernels, shards(): pl.pallas_call(functools.partial(correlate, 1.0 / (slabs * frames)), grid...  3.92 us
    pallas_call x1, Pallas kernels, shards(): pl.pallas_call(functools.partial(add_hops, slabs, frames), grid_spec=pltp...  1.62 us
  transfers between devices with their start and end apart: 6, of which 4 were waited for; matrix products, arithmetic and copies ran while one was open for 0% of the time, Pallas kernels for 0%

commit v1 on v0

v1 whole, which is shorter than its diff:
```python
import functools

import jax
import jax.numpy as jnp
import ml_dtypes
import numpy as np
from jax import lax
from jax.experimental import pallas as pl
from jax.experimental.pallas import tpu as pltpu
from jax.sharding import PartitionSpec as P

NCH = 4096
CH_DEV = 2
SUBLANES = 8
LANES = 128
CORES = 2
ROW_TILE = 16
FLAGGED = 1e30
MIB = 1 << 20
WIDTH = 1024
AHEAD = 2


def round_up(value, step):
    return -(-value // step) * step


def partner(index, distance, count):
    if count & (count - 1) == 0:
        return index ^ distance
    return (distance - index) % count


def exchange(value, axis, distance):
    count = lax.axis_size(axis)
    return lax.ppermute(value, axis, [(source, partner(source, distance, count)) for source in range(count)])


def slab_table(length, slabs, lowest):
    sample_ids = np.arange(length, dtype=np.int64)
    channel_ids = lowest + np.arange(slabs * CH_DEV, dtype=np.int64)
    angle = 2.0 * np.pi / length * (channel_ids[:, None] * sample_ids[None, :] % length)
    factor = np.sqrt(2.0 / length)
    both = np.stack([factor * np.cos(angle), -factor * np.sin(angle)], axis=0)
    by_slab = both.reshape(2, slabs, CH_DEV, length).transpose(1, 0, 2, 3).reshape(slabs, 2 * CH_DEV, length)
    return np.tile(by_slab, (1, SUBLANES // (2 * CH_DEV), 1)).astype(ml_dtypes.bfloat16)


def cut(length):
    widths = [WIDTH // 2] + [WIDTH] * (length // WIDTH - 1) + [WIDTH // 2] if length % WIDTH == 0 else [length]
    starts = np.cumsum([0] + widths)
    return [(int(start), width) for start, width in zip(starts, widths)]


def channelize(slabs, me_ref, samples_hbm, fir_hbm, table_hbm, flags_hbm, *rest):
    outs, (samples, fir, table, flags, weights, sums, total, chunk_sems, sems) = rest[:slabs], rest[slabs:]
    frames, inputs, length = samples.shape
    taps = fir.shape[0]
    group = 2 * CH_DEV
    per_slab = taps * group
    pack = SUBLANES // group
    chunks = cut(length)
    small = [
        pltpu.make_async_copy(source, target, sems.at[place])
        for place, (source, target) in enumerate(((fir_hbm, fir), (table_hbm, table), (flags_hbm, flags)))
    ]
    loads = [
        pltpu.make_async_copy(
            samples_hbm.at[:, :, pl.ds(start, width)], samples.at[:, :, pl.ds(start, width)], chunk_sems.at[place]
        )
        for place, (start, width) in enumerate(chunks)
    ]
    for copy in small + loads[:AHEAD]:
        copy.start()

    def make_weights(start, width):
        row_ids = lax.broadcasted_iota(jnp.int32, (SUBLANES, width), 0)
        columns = pl.ds(start, width)
        tables = [table[partner(me_ref[0], slot, slabs), :, columns].astype(jnp.float32) for slot in range(slabs)]
        for first in range(0, taps, 2 * pack):
            coefs = []
            for half in range(2):
                coef = None
                for place in range(pack):
                    tap = taps - 1 - (first + half * pack + place)
                    line = jnp.broadcast_to(fir[tap : tap + 1, columns], (SUBLANES, width))
                    coef = line if coef is None else jnp.where(row_ids >= place * group, line, coef)
                coefs.append(coef)
            for slot in range(slabs):
                rows = jnp.concatenate([coef * tables[slot] for coef in coefs], axis=0)
                weights[pl.ds(slot * per_slab + first * group, ROW_TILE), columns] = rows.astype(jnp.bfloat16)

    total[...] = jnp.zeros_like(total)
    for copy in small:
        copy.wait()
    for copy in loads[AHEAD:]:
        copy.start()
    make_weights(*chunks[0])
    for place, (start, width) in enumerate(chunks):
        loads[place].wait()
        columns = pl.ds(start, width)
        if place + 1 < len(chunks):
            make_weights(*chunks[place + 1])
        for frame in range(frames):
            before = sums[frame] if place else jnp.zeros(sums.shape[1:], jnp.float32)
            after = before + lax.dot_general(
                weights[:, columns],
                samples[frame, :, columns],
                (((1,), (1,)), ((), ())),
                preferred_element_type=jnp.float32,
            )
            if place + 1 < len(chunks):
                sums[frame] = after
                continue
            for slot in range(slabs):
                total[slot, pl.ds(frame * group, per_slab), :] += after[slot * per_slab : (slot + 1) * per_slab]

    good = jnp.broadcast_to(flags[...][:, None, :], (frames, group, inputs)).reshape(frames * group, inputs)
    own = frames * group
    for slot in range(slabs):
        total[slot, 0:own, :] = jnp.where(good == 0, FLAGGED, total[slot, 0:own, :])
        outs[slot][...] = total[slot].astype(outs[slot].dtype)


def add_hops(slabs, frames, me_ref, *rest):
    pieces, (out_ref, total) = rest[:slabs][::-1], rest[slabs:]
    group = 2 * CH_DEV
    total[...] = jnp.zeros_like(total)
    for slot in range(slabs):
        place = pl.multiple_of(partner(me_ref[0], slot, slabs) * (frames * group), SUBLANES)
        total[pl.ds(place, pieces[slot].shape[0]), :] += pieces[slot][...].astype(jnp.float32)
    value = total[0 : out_ref.shape[0], :]
    out_ref[...] = jnp.where(value > 0.5 * FLAGGED, 0.0, value).astype(out_ref.dtype)


def make_left(own_ref, left_ref):
    rows, inputs = own_ref.shape
    group = 2 * CH_DEV
    own = own_ref[...].astype(jnp.float32)
    row_ids = lax.broadcasted_iota(jnp.int32, own.shape, 0)
    is_real = row_ids % group < CH_DEV
    turned = jnp.where(is_real, pltpu.roll(own, rows - CH_DEV, 0), -pltpu.roll(own, CH_DEV, 0))
    for channel in range(CH_DEV):
        keep = row_ids % CH_DEV == channel
        for part, value in enumerate((own, turned)):
            place = (channel * 2 + part) * inputs
            left_ref[pl.ds(place, inputs), :] = jnp.where(keep, value, 0.0).T.astype(left_ref.dtype)


def multiply(scale, blocks, slots, me_ref, left_ref, pieces, out_hbm, parts, sems):
    copies = []
    inputs = parts.shape[3]
    for place, (slot, piece) in enumerate(zip(slots, pieces)):
        width = piece.shape[1]
        first = 0 if blocks == 1 else pl.multiple_of(partner(me_ref[0], slot, blocks) * width, LANES)
        for channel in range(CH_DEV):
            for part in range(2):
                rows = left_ref[pl.ds((channel * 2 + part) * inputs, inputs), :]
                parts[place, channel, part] = jnp.dot(rows, piece[...], preferred_element_type=jnp.float32) * scale
                copies.append(
                    pltpu.make_async_copy(
                        parts.at[place, channel, part],
                        out_hbm.at[channel, part, :, pl.ds(first, width)],
                        sems.at[place, channel, part],
                    )
                )
                copies[-1].start()
    for copy in copies:
        copy.wait()


def correlate_first(scale, blocks, slots, me_ref, own_ref, *rest):
    pieces, (out_hbm, left_ref, parts, sems) = rest[: len(slots)], rest[len(slots) :]
    make_left(own_ref, left_ref)
    multiply(scale, blocks, slots, me_ref, left_ref, pieces, out_hbm, parts, sems)


def correlate_rest(scale, blocks, slots, me_ref, left_ref, *rest):
    pieces, (_, out_hbm, parts, sems) = rest[: len(slots)], rest[len(slots) :]
    multiply(scale, blocks, slots, me_ref, left_ref, pieces, out_hbm, parts, sems)


def shards(samples, fir, flags):
    frames, inputs, length = samples.shape
    taps = fir.shape[0]
    slabs = lax.axis_size("tm")
    blocks = lax.axis_size("inp")
    group = 2 * CH_DEV
    window = frames + taps - 1
    rows = round_up(window * group, ROW_TILE)
    spectra_rows = slabs * frames * group
    table = jnp.asarray(slab_table(length, slabs, NCH // 4))
    my_slab = lax.axis_index("tm").astype(jnp.int32).reshape(1)
    my_block = lax.axis_index("inp").astype(jnp.int32).reshape(1)

    chunks = len(cut(length))
    sent = pl.pallas_call(
        functools.partial(channelize, slabs),
        in_specs=[pl.BlockSpec(memory_space=pltpu.SMEM)] + [pl.BlockSpec(memory_space=pltpu.HBM)] * 4,
        out_specs=[pl.BlockSpec(memory_space=pltpu.VMEM)] * slabs,
        scratch_shapes=[
            pltpu.VMEM(samples.shape, samples.dtype),
            pltpu.VMEM(fir.shape, fir.dtype),
            pltpu.VMEM(table.shape, table.dtype),
            pltpu.VMEM(flags.shape, flags.dtype),
            pltpu.VMEM((slabs * taps * group, length), jnp.bfloat16),
            pltpu.VMEM((frames, slabs * taps * group, inputs), jnp.float32),
            pltpu.VMEM((slabs, rows, inputs), jnp.float32),
            pltpu.SemaphoreType.DMA((chunks,)),
            pltpu.SemaphoreType.DMA((3,)),
        ],
        out_shape=[
            jax.ShapeDtypeStruct((rows, inputs), jnp.bfloat16 if slot else jnp.float32) for slot in range(slabs)
        ],
        compiler_params=pltpu.CompilerParams(vmem_limit_bytes=56 * MIB),
        name="channelize",
    )(my_slab, samples, fir, table, flags)

    arrived = {slot: exchange(sent[slot], "tm", slot) for slot in reversed(range(1, slabs))}
    pieces = [jnp.maximum(sent[0], -FLAGGED)] + [arrived[slot] for slot in range(1, slabs)]
    smem = pl.BlockSpec(memory_space=pltpu.SMEM)
    vmem = pl.BlockSpec(memory_space=pltpu.VMEM)
    hbm = pl.BlockSpec(memory_space=pltpu.HBM)
    spectra = pl.pallas_call(
        functools.partial(add_hops, slabs, frames),
        in_specs=[smem] + [vmem] * slabs,
        out_specs=vmem,
        scratch_shapes=[pltpu.VMEM((spectra_rows + rows, inputs), jnp.float32)],
        out_shape=jax.ShapeDtypeStruct((spectra_rows, inputs), jnp.bfloat16),
        compiler_params=pltpu.CompilerParams(vmem_limit_bytes=4 * MIB),
        name="add_hops",
    )(my_slab, *pieces[::-1])

    scale = 1.0 / (slabs * frames)
    out_shape = jax.ShapeDtypeStruct((CH_DEV, 2, inputs, blocks * inputs), jnp.float32)
    left_shape = jax.ShapeDtypeStruct((CH_DEV * 2 * inputs, spectra_rows), jnp.bfloat16)

    def scratch(count, width):
        return [pltpu.VMEM((count, CH_DEV, 2, inputs, width), jnp.float32), pltpu.SemaphoreType.DMA((count, CH_DEV, 2))]

    if inputs % LANES:
        columns = lax.all_gather(spectra, "inp", axis=1, tiled=True)
        return pl.pallas_call(
            functools.partial(correlate_first, scale, 1, (0,)),
            in_specs=[smem, vmem, vmem],
            out_specs=[hbm, vmem],
            out_shape=[out_shape, left_shape],
            scratch_shapes=scratch(1, blocks * inputs),
            compiler_params=pltpu.CompilerParams(vmem_limit_bytes=16 * MIB),
        name="correlate",
        )(my_block, spectra, columns)[0]

    slots = list(range(1, blocks))
    arrived = {slot: exchange(spectra, "inp", slot) for slot in reversed(slots)}
    early, late = slots[: CORES - 1], slots[CORES - 1 :]
    visibilities, left = pl.pallas_call(
        functools.partial(correlate_first, scale, blocks, [0] + early),
        in_specs=[smem, vmem, vmem] + [vmem] * len(early),
        out_specs=[hbm, vmem],
        out_shape=[out_shape, left_shape],
        scratch_shapes=scratch(1 + len(early), inputs),
        cost_estimate=pl.CostEstimate(flops=MIB << 7, bytes_accessed=2 * MIB, transcendentals=0),
        compiler_params=pltpu.CompilerParams(vmem_limit_bytes=16 * MIB),
        name="correlate_first",
    )(my_block, spectra, spectra, *[arrived[slot] for slot in early])
    return pl.pallas_call(
        functools.partial(correlate_rest, scale, blocks, late),
        in_specs=[smem, vmem] + [vmem] * len(late) + [hbm],
        out_specs=hbm,
        out_shape=out_shape,
        scratch_shapes=scratch(len(late), inputs),
        input_output_aliases={2 + len(late): 0},
        compiler_params=pltpu.CompilerParams(vmem_limit_bytes=16 * MIB),
        name="correlate_rest",
    )(my_block, left, *[arrived[slot] for slot in late], visibilities)


def solution(mesh):
    in_specs = (P(("grp", "tm"), "inp", None), P(), P(("grp", "tm"), "inp"))
    out_specs = P(("grp", "tm"), None, "inp", None)
    return jax.shard_map(shards, mesh=mesh, in_specs=in_specs, out_specs=out_specs, check_vma=False)
```

time: 44.4 us -> 31.8 us (0.72)
  Pallas kernels: 21.7 us -> 17 us
  local copies, waits for them, and re-layouts: 4.66 us -> 0 us
  waiting for transfers between devices: 10 us -> 5.7 us
  other arithmetic: 0 us -> 0.9 us
  starting transfers between devices: 7.48 us -> 7.98 us
    unnamed x20 -> x0, local copies, waits for them, and re-layouts: 4.66 us -> none
    pallas_call x3 -> x4, Pallas kernels: 21.7 us -> 17 us  [the longest x1 13.7 us: shards(): pl.pallas_call(functools.partial(channelize, slabs), in_specs=[pl.BlockSp...]
    ppermute x6, waiting for transfers between devices: 10 us -> 5.7 us  [exchange(): lax.ppermute(value, axis, [(source, partner(source, distance, count)) for...]
    max x0 -> x1, other arithmetic: none -> 0.9 us  [shards(): jnp.maximum(sent[0], -FLAGGED)]
    ppermute x6, starting transfers between devices: 7.48 us -> 7.98 us  [exchange(): lax.ppermute(value, axis, [(source, partner(source, distance, count)) for...]
  transfers between devices with their start and end apart: 6 -> 6, of which waited for: 4 -> 4; matrix products, arithmetic and copies ran while one was open for 0% -> 3% of each run, Pallas kernels for 0% -> 5%
where the time goes in v1:
time: 31.8 us; the launch traced here: 31.7 us
  Pallas kernels  17 us (53%)
  starting transfers between devices  7.98 us (25%)
  waiting for transfers between devices  5.7 us (18%)
  other arithmetic  0.9 us (3%)
    pallas_call x1, Pallas kernels, shards(): pl.pallas_call(functools.partial(channelize, slabs), in_specs=[pl.BlockSp...  13.7 us
    ppermute x6, starting transfers between devices, exchange(): lax.ppermute(value, axis, [(source, partner(source, distance, count)) for...  7.98 us
    ppermute x6, waiting for transfers between devices, exchange(): lax.ppermute(value, axis, [(source, partner(source, distance, count)) for...  5.7 us
    pallas_call x1, Pallas kernels, shards(): pl.pallas_call(functools.partial(correlate_first, scale, blocks, [0] + ea...  1.69 us
    pallas_call x1, Pallas kernels, shards(): pl.pallas_call(functools.partial(correlate_rest, scale, blocks, late), in...  1.59 us
    max x1, other arithmetic, shards(): jnp.maximum(sent[0], -FLAGGED)  0.9 us
  transfers between devices with their start and end apart: 6, of which 4 were waited for; matrix products, arithmetic and copies ran while one was open for 3% of the time, Pallas kernels for 5%

profile of v1, /device:TPU:0, one launch (start us, length us, event | category | flops | bytes accessed | tf_op | source)
XLA Modules:
  0.0 31.7 jit_solution(13136937982412153714)
XLA Ops:
  0.0 13.7 %channelize.1 = (f32[96,256]{1,0:T(8,128)}, bf16[96,256]{1,0:T(8,128)(2,1)}, bf16[96,256]{1,0:T(8,128)(2,1)}, bf16[96,256]{1,0:T(8,128)(2,1)}) custom-call(s32[1]{0:T(128)} %bitcast.1.me_ref, bf16[8,256,8192]{2,1,0:T(8,128)(2,1)} %samples_hbm.1, f32[16,8192]{1,0:T(8,128)} %fir_hbm.1, bf16[4,8,8192]{2,1,0:T(8,128)(2,1)} %constant.11.clone.table_hbm, ...), custom_call_target="tpu_custom_call" | custom-call | tf_op jit(solution)/shard_map/channelize/pallas_call | solution.py:197
  13.7 5.1 %collective-permute-start = (bf16[96,256]{1,0:T(8,128)(2,1)}, bf16[96,256]{1,0:T(8,128)(2,1)S(1)}, u32[]{:S(2)}, u32[]{:S(2)}) collective-permute-start(bf16[96,256]{1,0:T(8,128)(2,1)} %get-tuple-element.11), channel_id=1, source_target_pairs={{0,3},{1,2},{2,1},{3,0},{4,7},{5,6},{6,5},{7,4},{8,11},{9,10},{10,... | collective-permute-start | bytes 147464 | tf_op jit(solution)/shard_map/ppermute | solution.py:36
  18.8 0.0 collective-permute-start.1
  18.8 0.6 %collective-permute-start.2 = (bf16[96,256]{1,0:T(8,128)(2,1)}, bf16[96,256]{1,0:T(8,128)(2,1)S(1)}, u32[]{:S(2)}, u32[]{:S(2)}) collective-permute-start(bf16[96,256]{1,0:T(8,128)(2,1)} %get-tuple-element.13), channel_id=1, source_target_pairs={{0,1},{1,0},{2,3},{3,2},{4,5},{5,4},{6,7},{7,6},{8,9},{9,8},{10,11... | collective-permute-start | bytes 147464 | tf_op jit(solution)/shard_map/ppermute | solution.py:36
  19.5 0.9 %broadcast_maximum_fusion.rest_3_ = f32[96,256]{1,0:T(8,128)S(1)} fusion(f32[96,256]{1,0:T(8,128)} %get-tuple-element.14), kind=kLoop, calls=%fused_computation | loop fusion | flops 24576 | bytes 196608 | tf_op jit(solution)/shard_map/max | solution.py:220
  20.4 0.9 %collective-permute-done.rest_0_ = bf16[96,256]{1,0:T(8,128)(2,1)S(1)} collective-permute-done((bf16[96,256]{1,0:T(8,128)(2,1)}, bf16[96,256]{1,0:T(8,128)(2,1)S(1)}, u32[]{:S(2)}, u32[]{:S(2)}) %collective-permute-start) | collective-permute-done | bytes 49184 | tf_op jit(solution)/shard_map/ppermute | solution.py:36
  21.3 2.7 %collective-permute-done.1.rest_1_ = bf16[96,256]{1,0:T(8,128)(2,1)S(1)} collective-permute-done((bf16[96,256]{1,0:T(8,128)(2,1)}, bf16[96,256]{1,0:T(8,128)(2,1)S(1)}, u32[]{:S(2)}, u32[]{:S(2)}) %collective-permute-start.1) | collective-permute-done | bytes 49184 | tf_op jit(solution)/shard_map/ppermute | solution.py:36
  24.0 0.0 collective-permute-done.2.rest_2_
  24.0 0.1 add_hops.1.own_ref.rest_0_
  24.1 0.1 collective-permute-start.3
  24.2 1.6 %collective-permute-start.5 = (bf16[128,256]{1,0:T(8,128)(2,1)S(1)}, bf16[128,256]{1,0:T(8,128)(2,1)S(1)}, u32[]{:S(2)}, u32[]{:S(2)}) collective-permute-start(bf16[128,256]{1,0:T(8,128)(2,1)S(1)} %add_hops.1.own_ref.rest_0_), channel_id=1, source_target_pairs={{0,12},{4,8},{8,4},{12,0},{1,13},{5,9},{9,5},{13,1},{2,14},{6,10},... | collective-permute-start | bytes 196616 | tf_op jit(solution)/shard_map/ppermute | solution.py:36
  25.8 0.5 %collective-permute-start.4 = (bf16[128,256]{1,0:T(8,128)(2,1)S(1)}, bf16[128,256]{1,0:T(8,128)(2,1)S(1)}, u32[]{:S(2)}, u32[]{:S(2)}) collective-permute-start(bf16[128,256]{1,0:T(8,128)(2,1)S(1)} %add_hops.1.own_ref.rest_0_), channel_id=1, source_target_pairs={{0,8},{4,12},{8,0},{12,4},{1,9},{5,13},{9,1},{13,5},{2,10},{6,14},... | collective-permute-start | bytes 196616 | tf_op jit(solution)/shard_map/ppermute | solution.py:36
  26.3 0.0 collective-permute-done.3.rest_1_
  26.3 1.7 %correlate_first.1 = (f32[2,2,256,1024]{3,2,1,0:T(8,128)}, bf16[1024,128]{1,0:T(8,128)(2,1)S(1)}) custom-call(s32[1]{0:T(128)} %bitcast.me_ref, bf16[128,256]{1,0:T(8,128)(2,1)S(1)} %add_hops.1.own_ref.rest_0_, bf16[128,256]{1,0:T(8,128)(2,1)S(1)} %add_hops.1.own_ref.rest_0_, bf16[128,256]{1,0:T(8,128)(2,1)S(1)} %collective-permute-done.3.rest_1_), custom_call_target="tpu_custom_call" | custom-call | flops 134217728 | bytes 2097152 | tf_op jit(solution)/shard_map/correlate_first/pallas_call | solution.py:256
  28.0 0.2 collective-permute-done.5.rest_1_
  28.2 1.8 %collective-permute-done.4.rest_0_ = bf16[128,256]{1,0:T(8,128)(2,1)S(1)} collective-permute-done((bf16[128,256]{1,0:T(8,128)(2,1)S(1)}, bf16[128,256]{1,0:T(8,128)(2,1)S(1)}, u32[]{:S(2)}, u32[]{:S(2)}) %collective-permute-start.4) | collective-permute-done | bytes 65568 | tf_op jit(solution)/shard_map/ppermute | solution.py:36
  30.1 1.6 %correlate_rest.1 = f32[2,2,256,1024]{3,2,1,0:T(8,128)} custom-call(s32[1]{0:T(128)} %bitcast.me_ref, bf16[1024,128]{1,0:T(8,128)(2,1)S(1)} %get-tuple-element.15.left_ref, bf16[128,256]{1,0:T(8,128)(2,1)S(1)} %collective-permute-done.4.rest_0_, bf16[128,256]{1,0:T(8,128)(2,1)S(1)} %collective-permute-done.5.rest_1_, ...), custom_call_target="tpu_custom_call", output_to_operand_aliasing={{}: (4, {})} | custom-call | tf_op jit(solution)/shard_map/correlate_rest/pallas_call | solution.py:266
Async XLA Ops:
  13.7 7.6 %collective-permute-start = (bf16[96,256]{1,0:T(8,128)(2,1)}, bf16[96,256]{1,0:T(8,128)(2,1)S(1)}, u32[]{:S(2)}, u32[]{:S(2)}) collective-permute-start(bf16[96,256]{1,0:T(8,128)(2,1)} %get-tuple-element.11), channel_id=1, source_target_pairs={{0,3},{1,2},{2,1},{3,0},{4,7},{5,6},{6,5},{7,4},{8,11},{9,10},{10,... | collective-permute-start | bytes 147464 | tf_op jit(solution)/shard_map/ppermute | solution.py:36
  18.8 5.2 %collective-permute-start.1 = (bf16[96,256]{1,0:T(8,128)(2,1)}, bf16[96,256]{1,0:T(8,128)(2,1)S(1)}, u32[]{:S(2)}, u32[]{:S(2)}) collective-permute-start(bf16[96,256]{1,0:T(8,128)(2,1)} %get-tuple-element.12), channel_id=1, source_target_pairs={{0,2},{1,3},{2,0},{3,1},{4,6},{5,7},{6,4},{7,5},{8,10},{9,11},{10,... | collective-permute-start | bytes 147464 | tf_op jit(solution)/shard_map/ppermute | solution.py:36
  18.8 5.2 %collective-permute-start.2 = (bf16[96,256]{1,0:T(8,128)(2,1)}, bf16[96,256]{1,0:T(8,128)(2,1)S(1)}, u32[]{:S(2)}, u32[]{:S(2)}) collective-permute-start(bf16[96,256]{1,0:T(8,128)(2,1)} %get-tuple-element.13), channel_id=1, source_target_pairs={{0,1},{1,0},{2,3},{3,2},{4,5},{5,4},{6,7},{7,6},{8,9},{9,8},{10,11... | collective-permute-start | bytes 147464 | tf_op jit(solution)/shard_map/ppermute | solution.py:36
  24.1 2.2 %collective-permute-start.3 = (bf16[128,256]{1,0:T(8,128)(2,1)S(1)}, bf16[128,256]{1,0:T(8,128)(2,1)S(1)}, u32[]{:S(2)}, u32[]{:S(2)}) collective-permute-start(bf16[128,256]{1,0:T(8,128)(2,1)S(1)} %add_hops.1.own_ref.rest_0_), channel_id=1, source_target_pairs={{0,4},{4,0},{8,12},{12,8},{1,5},{5,1},{9,13},{13,9},{2,6},{6,2},{1... | collective-permute-start | bytes 196616 | tf_op jit(solution)/shard_map/ppermute | solution.py:36
  24.2 4.0 %collective-permute-start.5 = (bf16[128,256]{1,0:T(8,128)(2,1)S(1)}, bf16[128,256]{1,0:T(8,128)(2,1)S(1)}, u32[]{:S(2)}, u32[]{:S(2)}) collective-permute-start(bf16[128,256]{1,0:T(8,128)(2,1)S(1)} %add_hops.1.own_ref.rest_0_), channel_id=1, source_target_pairs={{0,12},{4,8},{8,4},{12,0},{1,13},{5,9},{9,5},{13,1},{2,14},{6,10},... | collective-permute-start | bytes 196616 | tf_op jit(solution)/shard_map/ppermute | solution.py:36
  25.8 4.3 %collective-permute-start.4 = (bf16[128,256]{1,0:T(8,128)(2,1)S(1)}, bf16[128,256]{1,0:T(8,128)(2,1)S(1)}, u32[]{:S(2)}, u32[]{:S(2)}) collective-permute-start(bf16[128,256]{1,0:T(8,128)(2,1)S(1)} %add_hops.1.own_ref.rest_0_), channel_id=1, source_target_pairs={{0,8},{4,12},{8,0},{12,4},{1,9},{5,13},{9,1},{13,5},{2,10},{6,14},... | collective-permute-start | bytes 196616 | tf_op jit(solution)/shard_map/ppermute | solution.py:36

commit v2 on v1

--- a/solution.py
+++ b/solution.py
@@ -263,16 +263,18 @@
         compiler_params=pltpu.CompilerParams(vmem_limit_bytes=16 * MIB),
         name="correlate_first",
     )(my_block, spectra, spectra, *[arrived[slot] for slot in early])
-    return pl.pallas_call(
-        functools.partial(correlate_rest, scale, blocks, late),
-        in_specs=[smem, vmem] + [vmem] * len(late) + [hbm],
-        out_specs=hbm,
-        out_shape=out_shape,
-        scratch_shapes=scratch(len(late), inputs),
-        input_output_aliases={2 + len(late): 0},
-        compiler_params=pltpu.CompilerParams(vmem_limit_bytes=16 * MIB),
-        name="correlate_rest",
-    )(my_block, left, *[arrived[slot] for slot in late], visibilities)
+    for slot in reversed(late):
+        visibilities = pl.pallas_call(
+            functools.partial(correlate_rest, scale, blocks, [slot]),
+            in_specs=[smem, vmem, vmem, hbm],
+            out_specs=hbm,
+            out_shape=out_shape,
+            scratch_shapes=scratch(1, inputs),
+            input_output_aliases={3: 0},
+            compiler_params=pltpu.CompilerParams(vmem_limit_bytes=16 * MIB),
+            name="correlate_rest",
+        )(my_block, left, arrived[slot], visibilities)
+    return visibilities
 
 
 def solution(mesh):

time: 31.8 us -> 31.4 us (0.987)
  waiting for transfers between devices: 5.7 us -> 4.48 us
  Pallas kernels: 17 us -> 17.9 us
    ppermute x6, waiting for transfers between devices: 5.7 us -> 4.48 us  [exchange(): lax.ppermute(value, axis, [(source, partner(source, distance, count)) for...]
    pallas_call x1 -> x2, Pallas kernels: 1.59 us -> 2.42 us  [shards(): pl.pallas_call(functools.partial(correlate_rest, scale, blocks, [slot]),...]
  transfers between devices with their start and end apart: 6 -> 6, of which waited for: 4 -> 4; matrix products, arithmetic and copies ran while one was open for 3% -> 3% of each run, Pallas kernels for 5% -> 9%
where the time goes in v2:
time: 31.4 us; the launch traced here: 31.3 us
  Pallas kernels  17.9 us (57%)
  starting transfers between devices  7.98 us (25%)
  waiting for transfers between devices  4.48 us (14%)
  other arithmetic  0.9 us (3%)
    pallas_call x1, Pallas kernels, shards(): pl.pallas_call(functools.partial(channelize, slabs), in_specs=[pl.BlockSp...  13.7 us
    ppermute x6, starting transfers between devices, exchange(): lax.ppermute(value, axis, [(source, partner(source, distance, count)) for...  7.98 us
    ppermute x6, waiting for transfers between devices, exchange(): lax.ppermute(value, axis, [(source, partner(source, distance, count)) for...  4.48 us
    pallas_call x2, Pallas kernels, shards(): pl.pallas_call(functools.partial(correlate_rest, scale, blocks, [slot]),...  2.42 us
    pallas_call x1, Pallas kernels, shards(): pl.pallas_call(functools.partial(correlate_first, scale, blocks, [0] + ea...  1.69 us
    max x1, other arithmetic, shards(): jnp.maximum(sent[0], -FLAGGED)  0.9 us
  transfers between devices with their start and end apart: 6, of which 4 were waited for; matrix products, arithmetic and copies ran while one was open for 3% of the time, Pallas kernels for 9%

profile of v2, /device:TPU:0, one launch (start us, length us, event | category | flops | bytes accessed | tf_op | source)
XLA Modules:
  0.0 31.3 jit_solution(11848320917189079741)
XLA Ops:
  0.0 13.7 %channelize.1 = (f32[96,256]{1,0:T(8,128)}, bf16[96,256]{1,0:T(8,128)(2,1)}, bf16[96,256]{1,0:T(8,128)(2,1)}, bf16[96,256]{1,0:T(8,128)(2,1)}) custom-call(s32[1]{0:T(128)} %bitcast.1.me_ref, bf16[8,256,8192]{2,1,0:T(8,128)(2,1)} %samples_hbm.1, f32[16,8192]{1,0:T(8,128)} %fir_hbm.1, bf16[4,8,8192]{2,1,0:T(8,128)(2,1)} %constant.11.clone.table_hbm, ...), custom_call_target="tpu_custom_call" | custom-call | tf_op jit(solution)/shard_map/channelize/pallas_call | solution.py:197
  13.7 5.1 %collective-permute-start = (bf16[96,256]{1,0:T(8,128)(2,1)}, bf16[96,256]{1,0:T(8,128)(2,1)S(1)}, u32[]{:S(2)}, u32[]{:S(2)}) collective-permute-start(bf16[96,256]{1,0:T(8,128)(2,1)} %get-tuple-element.11), channel_id=1, source_target_pairs={{0,3},{1,2},{2,1},{3,0},{4,7},{5,6},{6,5},{7,4},{8,11},{9,10},{10,... | collective-permute-start | bytes 147464 | tf_op jit(solution)/shard_map/ppermute | solution.py:36
  18.8 0.0 collective-permute-start.1
  18.8 0.6 %collective-permute-start.2 = (bf16[96,256]{1,0:T(8,128)(2,1)}, bf16[96,256]{1,0:T(8,128)(2,1)S(1)}, u32[]{:S(2)}, u32[]{:S(2)}) collective-permute-start(bf16[96,256]{1,0:T(8,128)(2,1)} %get-tuple-element.13), channel_id=1, source_target_pairs={{0,1},{1,0},{2,3},{3,2},{4,5},{5,4},{6,7},{7,6},{8,9},{9,8},{10,11... | collective-permute-start | bytes 147464 | tf_op jit(solution)/shard_map/ppermute | solution.py:36
  19.5 0.9 %broadcast_maximum_fusion.rest_3_ = f32[96,256]{1,0:T(8,128)S(1)} fusion(f32[96,256]{1,0:T(8,128)} %get-tuple-element.14), kind=kLoop, calls=%fused_computation | loop fusion | flops 24576 | bytes 196608 | tf_op jit(solution)/shard_map/max | solution.py:220
  20.4 0.9 %collective-permute-done.rest_0_ = bf16[96,256]{1,0:T(8,128)(2,1)S(1)} collective-permute-done((bf16[96,256]{1,0:T(8,128)(2,1)}, bf16[96,256]{1,0:T(8,128)(2,1)S(1)}, u32[]{:S(2)}, u32[]{:S(2)}) %collective-permute-start) | collective-permute-done | bytes 49184 | tf_op jit(solution)/shard_map/ppermute | solution.py:36
  21.3 2.7 %collective-permute-done.1.rest_1_ = bf16[96,256]{1,0:T(8,128)(2,1)S(1)} collective-permute-done((bf16[96,256]{1,0:T(8,128)(2,1)}, bf16[96,256]{1,0:T(8,128)(2,1)S(1)}, u32[]{:S(2)}, u32[]{:S(2)}) %collective-permute-start.1) | collective-permute-done | bytes 49184 | tf_op jit(solution)/shard_map/ppermute | solution.py:36
  24.0 0.0 collective-permute-done.2.rest_2_
  24.0 0.1 add_hops.1.own_ref.rest_0_
  24.1 0.1 collective-permute-start.3
  24.2 1.6 %collective-permute-start.5 = (bf16[128,256]{1,0:T(8,128)(2,1)S(1)}, bf16[128,256]{1,0:T(8,128)(2,1)S(1)}, u32[]{:S(2)}, u32[]{:S(2)}) collective-permute-start(bf16[128,256]{1,0:T(8,128)(2,1)S(1)} %add_hops.1.own_ref.rest_0_), channel_id=1, source_target_pairs={{0,12},{4,8},{8,4},{12,0},{1,13},{5,9},{9,5},{13,1},{2,14},{6,10},... | collective-permute-start | bytes 196616 | tf_op jit(solution)/shard_map/ppermute | solution.py:36
  25.8 0.5 %collective-permute-start.4 = (bf16[128,256]{1,0:T(8,128)(2,1)S(1)}, bf16[128,256]{1,0:T(8,128)(2,1)S(1)}, u32[]{:S(2)}, u32[]{:S(2)}) collective-permute-start(bf16[128,256]{1,0:T(8,128)(2,1)S(1)} %add_hops.1.own_ref.rest_0_), channel_id=1, source_target_pairs={{0,8},{4,12},{8,0},{12,4},{1,9},{5,13},{9,1},{13,5},{2,10},{6,14},... | collective-permute-start | bytes 196616 | tf_op jit(solution)/shard_map/ppermute | solution.py:36
  26.3 0.0 collective-permute-done.3.rest_1_
  26.3 1.7 %correlate_first.1 = (f32[2,2,256,1024]{3,2,1,0:T(8,128)}, bf16[1024,128]{1,0:T(8,128)(2,1)S(1)}) custom-call(s32[1]{0:T(128)} %bitcast.me_ref, bf16[128,256]{1,0:T(8,128)(2,1)S(1)} %add_hops.1.own_ref.rest_0_, bf16[128,256]{1,0:T(8,128)(2,1)S(1)} %add_hops.1.own_ref.rest_0_, bf16[128,256]{1,0:T(8,128)(2,1)S(1)} %collective-permute-done.3.rest_1_), custom_call_target="tpu_custom_call" | custom-call | flops 134217728 | bytes 2097152 | tf_op jit(solution)/shard_map/correlate_first/pallas_call | solution.py:256
  28.0 0.2 collective-permute-done.5.rest_0_
  28.2 1.2 %correlate_rest.2.rest_1_ = f32[2,2,256,1024]{3,2,1,0:T(8,128)} custom-call(s32[1]{0:T(128)} %bitcast.me_ref, bf16[1024,128]{1,0:T(8,128)(2,1)S(1)} %get-tuple-element.15.left_ref, bf16[128,256]{1,0:T(8,128)(2,1)S(1)} %collective-permute-done.5.rest_0_, f32[2,2,256,1024]{3,2,1,0:T(8,128)} %get-tuple-element.16.rest_1_), custom_call_target="tpu_custom_call", output_to_operand_aliasing={{}: (3, {})} | custom-call | tf_op jit(solution)/shard_map/correlate_rest/pallas_call | solution.py:267
  29.4 0.6 %collective-permute-done.4.rest_0_ = bf16[128,256]{1,0:T(8,128)(2,1)S(1)} collective-permute-done((bf16[128,256]{1,0:T(8,128)(2,1)S(1)}, bf16[128,256]{1,0:T(8,128)(2,1)S(1)}, u32[]{:S(2)}, u32[]{:S(2)}) %collective-permute-start.4) | collective-permute-done | bytes 65568 | tf_op jit(solution)/shard_map/ppermute | solution.py:36
  30.1 1.2 %correlate_rest.3 = f32[2,2,256,1024]{3,2,1,0:T(8,128)} custom-call(s32[1]{0:T(128)} %bitcast.me_ref, bf16[1024,128]{1,0:T(8,128)(2,1)S(1)} %get-tuple-element.15.left_ref, bf16[128,256]{1,0:T(8,128)(2,1)S(1)} %collective-permute-done.4.rest_0_, f32[2,2,256,1024]{3,2,1,0:T(8,128)} %correlate_rest.2.rest_1_), custom_call_target="tpu_custom_call", output_to_operand_aliasing={{}: (3, {})} | custom-call | tf_op jit(solution)/shard_map/correlate_rest/pallas_call | solution.py:267
Async XLA Ops:
  13.7 7.6 %collective-permute-start = (bf16[96,256]{1,0:T(8,128)(2,1)}, bf16[96,256]{1,0:T(8,128)(2,1)S(1)}, u32[]{:S(2)}, u32[]{:S(2)}) collective-permute-start(bf16[96,256]{1,0:T(8,128)(2,1)} %get-tuple-element.11), channel_id=1, source_target_pairs={{0,3},{1,2},{2,1},{3,0},{4,7},{5,6},{6,5},{7,4},{8,11},{9,10},{10,... | collective-permute-start | bytes 147464 | tf_op jit(solution)/shard_map/ppermute | solution.py:36
  18.8 5.2 %collective-permute-start.1 = (bf16[96,256]{1,0:T(8,128)(2,1)}, bf16[96,256]{1,0:T(8,128)(2,1)S(1)}, u32[]{:S(2)}, u32[]{:S(2)}) collective-permute-start(bf16[96,256]{1,0:T(8,128)(2,1)} %get-tuple-element.12), channel_id=1, source_target_pairs={{0,2},{1,3},{2,0},{3,1},{4,6},{5,7},{6,4},{7,5},{8,10},{9,11},{10,... | collective-permute-start | bytes 147464 | tf_op jit(solution)/shard_map/ppermute | solution.py:36
  18.8 5.2 %collective-permute-start.2 = (bf16[96,256]{1,0:T(8,128)(2,1)}, bf16[96,256]{1,0:T(8,128)(2,1)S(1)}, u32[]{:S(2)}, u32[]{:S(2)}) collective-permute-start(bf16[96,256]{1,0:T(8,128)(2,1)} %get-tuple-element.13), channel_id=1, source_target_pairs={{0,1},{1,0},{2,3},{3,2},{4,5},{5,4},{6,7},{7,6},{8,9},{9,8},{10,11... | collective-permute-start | bytes 147464 | tf_op jit(solution)/shard_map/ppermute | solution.py:36
  24.1 2.2 %collective-permute-start.3 = (bf16[128,256]{1,0:T(8,128)(2,1)S(1)}, bf16[128,256]{1,0:T(8,128)(2,1)S(1)}, u32[]{:S(2)}, u32[]{:S(2)}) collective-permute-start(bf16[128,256]{1,0:T(8,128)(2,1)S(1)} %add_hops.1.own_ref.rest_0_), channel_id=1, source_target_pairs={{0,4},{4,0},{8,12},{12,8},{1,5},{5,1},{9,13},{13,9},{2,6},{6,2},{1... | collective-permute-start | bytes 196616 | tf_op jit(solution)/shard_map/ppermute | solution.py:36
  24.2 4.0 %collective-permute-start.5 = (bf16[128,256]{1,0:T(8,128)(2,1)S(1)}, bf16[128,256]{1,0:T(8,128)(2,1)S(1)}, u32[]{:S(2)}, u32[]{:S(2)}) collective-permute-start(bf16[128,256]{1,0:T(8,128)(2,1)S(1)} %add_hops.1.own_ref.rest_0_), channel_id=1, source_target_pairs={{0,12},{4,8},{8,4},{12,0},{1,13},{5,9},{9,5},{13,1},{2,14},{6,10},... | collective-permute-start | bytes 196616 | tf_op jit(solution)/shard_map/ppermute | solution.py:36
  25.8 4.3 %collective-permute-start.4 = (bf16[128,256]{1,0:T(8,128)(2,1)S(1)}, bf16[128,256]{1,0:T(8,128)(2,1)S(1)}, u32[]{:S(2)}, u32[]{:S(2)}) collective-permute-start(bf16[128,256]{1,0:T(8,128)(2,1)S(1)} %add_hops.1.own_ref.rest_0_), channel_id=1, source_target_pairs={{0,8},{4,12},{8,0},{12,4},{1,9},{5,13},{9,1},{13,5},{2,10},{6,14},... | collective-permute-start | bytes 196616 | tf_op jit(solution)/shard_map/ppermute | solution.py:36

commit v3 on v2

--- a/solution.py
+++ b/solution.py
@@ -31,6 +31,19 @@
     return (distance - index) % count
 
 
+def routes(count):
+    if count == 4:
+        return [(0, 1, 2, 3), (1, 0, 3, 2), (3, 2, 0, 1), (2, 3, 1, 0)]
+    return [tuple(partner(source, slot, count) for source in range(count)) for slot in range(count)]
+
+
+def pick(values, index):
+    result = jnp.int32(values[0])
+    for place in range(1, len(values)):
+        result = jnp.where(index == place, jnp.int32(values[place]), result)
+    return result
+
+
 def exchange(value, axis, distance):
     count = lax.axis_size(axis)
     return lax.ppermute(value, axis, [(source, partner(source, distance, count)) for source in range(count)])
@@ -60,6 +73,7 @@
     per_slab = taps * group
     pack = SUBLANES // group
     chunks = cut(length)
+    targets = routes(slabs)
     small = [
         pltpu.make_async_copy(source, target, sems.at[place])
         for place, (source, target) in enumerate(((fir_hbm, fir), (table_hbm, table), (flags_hbm, flags)))
@@ -76,7 +90,7 @@
     def make_weights(start, width):
         row_ids = lax.broadcasted_iota(jnp.int32, (SUBLANES, width), 0)
         columns = pl.ds(start, width)
-        tables = [table[partner(me_ref[0], slot, slabs), :, columns].astype(jnp.float32) for slot in range(slabs)]
+        tables = [table[pick(targets[slot], me_ref[0]), :, columns].astype(jnp.float32) for slot in range(slabs)]
         for first in range(0, taps, 2 * pack):
             coefs = []
             for half in range(2):
@@ -125,9 +139,11 @@
 def add_hops(slabs, frames, me_ref, *rest):
     pieces, (out_ref, total) = rest[:slabs][::-1], rest[slabs:]
     group = 2 * CH_DEV
+    targets = routes(slabs)
     total[...] = jnp.zeros_like(total)
     for slot in range(slabs):
-        place = pl.multiple_of(partner(me_ref[0], slot, slabs) * (frames * group), SUBLANES)
+        source = pick([targets[slot].index(place) for place in range(slabs)], me_ref[0])
+        place = pl.multiple_of(source * (frames * group), SUBLANES)
         total[pl.ds(place, pieces[slot].shape[0]), :] += pieces[slot][...].astype(jnp.float32)
     value = total[0 : out_ref.shape[0], :]
     out_ref[...] = jnp.where(value > 0.5 * FLAGGED, 0.0, value).astype(out_ref.dtype)
@@ -216,7 +232,9 @@
         name="channelize",
     )(my_slab, samples, fir, table, flags)
 
-    arrived = {slot: exchange(sent[slot], "tm", slot) for slot in reversed(range(1, slabs))}
+    arrived = {
+        slot: lax.ppermute(sent[slot], "tm", list(enumerate(routes(slabs)[slot]))) for slot in reversed(range(1, slabs))
+    }
     pieces = [jnp.maximum(sent[0], -FLAGGED)] + [arrived[slot] for slot in range(1, slabs)]
     smem = pl.BlockSpec(memory_space=pltpu.SMEM)
     vmem = pl.BlockSpec(memory_space=pltpu.VMEM)

time: 31.4 us -> 31 us (0.987)
    ppermute x6 -> x3, starting transfers between devices: 7.98 us -> 2.21 us  [exchange(): lax.ppermute(value, axis, [(source, partner(source, distance, count)) for...]
    ppermute x0 -> x3, starting transfers between devices: none -> 5.68 us  [shards(): lax.ppermute(sent[slot], 'tm', list(enumerate(routes(slabs)[slot])))]
    ppermute x6 -> x3, waiting for transfers between devices: 4.48 us -> 0.84 us  [exchange(): lax.ppermute(value, axis, [(source, partner(source, distance, count)) for...]
    ppermute x0 -> x3, waiting for transfers between devices: none -> 3.33 us  [shards(): lax.ppermute(sent[slot], 'tm', list(enumerate(routes(slabs)[slot])))]
  transfers between devices with their start and end apart: 6 -> 6, of which waited for: 4 -> 5; matrix products, arithmetic and copies ran while one was open for 3% -> 3% of each run, Pallas kernels for 9% -> 9%
where the time goes in v3:
time: 31 us; the launch traced here: 30.9 us
  Pallas kernels  17.9 us (58%)
  starting transfers between devices  7.89 us (25%)
  waiting for transfers between devices  4.17 us (13%)
  other arithmetic  0.9 us (3%)
    pallas_call x1, Pallas kernels, shards(): pl.pallas_call(functools.partial(channelize, slabs), in_specs=[pl.BlockSp...  13.7 us
    ppermute x3, starting transfers between devices, shards(): lax.ppermute(sent[slot], 'tm', list(enumerate(routes(slabs)[slot])))  5.68 us
    ppermute x3, waiting for transfers between devices, shards(): lax.ppermute(sent[slot], 'tm', list(enumerate(routes(slabs)[slot])))  3.33 us
    pallas_call x2, Pallas kernels, shards(): pl.pallas_call(functools.partial(correlate_rest, scale, blocks, [slot]),...  2.42 us
    ppermute x3, starting transfers between devices, exchange(): lax.ppermute(value, axis, [(source, partner(source, distance, count)) for...  2.21 us
    pallas_call x1, Pallas kernels, shards(): pl.pallas_call(functools.partial(correlate_first, scale, blocks, [0] + ea...  1.69 us
    max x1, other arithmetic, shards(): jnp.maximum(sent[0], -FLAGGED)  0.9 us
    ppermute x3, waiting for transfers between devices, exchange(): lax.ppermute(value, axis, [(source, partner(source, distance, count)) for...  0.84 us
  transfers between devices with their start and end apart: 6, of which 5 were waited for; matrix products, arithmetic and copies ran while one was open for 3% of the time, Pallas kernels for 9%

profile of v3, /device:TPU:0, one launch (start us, length us, event | category | flops | bytes accessed | tf_op | source)
XLA Modules:
  0.0 30.9 jit_solution(3331263826839988390)
XLA Ops:
  0.0 13.7 %channelize.1 = (f32[96,256]{1,0:T(8,128)}, bf16[96,256]{1,0:T(8,128)(2,1)}, bf16[96,256]{1,0:T(8,128)(2,1)}, bf16[96,256]{1,0:T(8,128)(2,1)}) custom-call(s32[1]{0:T(128)} %bitcast.1.me_ref, bf16[8,256,8192]{2,1,0:T(8,128)(2,1)} %samples_hbm.1, f32[16,8192]{1,0:T(8,128)} %fir_hbm.1, bf16[4,8,8192]{2,1,0:T(8,128)(2,1)} %constant.11.clone.table_hbm, ...), custom_call_target="tpu_custom_call" | custom-call | tf_op jit(solution)/shard_map/channelize/pallas_call | solution.py:213
  13.7 4.1 %collective-permute-start = (bf16[96,256]{1,0:T(8,128)(2,1)}, bf16[96,256]{1,0:T(8,128)(2,1)S(1)}, u32[]{:S(2)}, u32[]{:S(2)}) collective-permute-start(bf16[96,256]{1,0:T(8,128)(2,1)} %get-tuple-element.11), channel_id=1, source_target_pairs={{0,2},{1,3},{2,1},{3,0},{4,6},{5,7},{6,5},{7,4},{8,10},{9,11},{10,... | collective-permute-start | bytes 147464 | tf_op jit(solution)/shard_map/ppermute | solution.py:236
  17.8 1.1 %collective-permute-start.1 = (bf16[96,256]{1,0:T(8,128)(2,1)}, bf16[96,256]{1,0:T(8,128)(2,1)S(1)}, u32[]{:S(2)}, u32[]{:S(2)}) collective-permute-start(bf16[96,256]{1,0:T(8,128)(2,1)} %get-tuple-element.12), channel_id=1, source_target_pairs={{0,3},{1,2},{2,0},{3,1},{4,7},{5,6},{6,4},{7,5},{8,11},{9,10},{10,... | collective-permute-start | bytes 147464 | tf_op jit(solution)/shard_map/ppermute | solution.py:236
  18.9 0.5 %collective-permute-start.2 = (bf16[96,256]{1,0:T(8,128)(2,1)}, bf16[96,256]{1,0:T(8,128)(2,1)S(1)}, u32[]{:S(2)}, u32[]{:S(2)}) collective-permute-start(bf16[96,256]{1,0:T(8,128)(2,1)} %get-tuple-element.13), channel_id=1, source_target_pairs={{0,1},{1,0},{2,3},{3,2},{4,5},{5,4},{6,7},{7,6},{8,9},{9,8},{10,11... | collective-permute-start | bytes 147464 | tf_op jit(solution)/shard_map/ppermute | solution.py:236
  19.4 0.9 %broadcast_maximum_fusion.rest_3_ = f32[96,256]{1,0:T(8,128)S(1)} fusion(f32[96,256]{1,0:T(8,128)} %get-tuple-element.14), kind=kLoop, calls=%fused_computation | loop fusion | flops 24576 | bytes 196608 | tf_op jit(solution)/shard_map/max | solution.py:238
  20.3 0.9 %collective-permute-done.rest_0_ = bf16[96,256]{1,0:T(8,128)(2,1)S(1)} collective-permute-done((bf16[96,256]{1,0:T(8,128)(2,1)}, bf16[96,256]{1,0:T(8,128)(2,1)S(1)}, u32[]{:S(2)}, u32[]{:S(2)}) %collective-permute-start) | collective-permute-done | bytes 49184 | tf_op jit(solution)/shard_map/ppermute | solution.py:236
  21.1 2.0 %collective-permute-done.1.rest_1_ = bf16[96,256]{1,0:T(8,128)(2,1)S(1)} collective-permute-done((bf16[96,256]{1,0:T(8,128)(2,1)}, bf16[96,256]{1,0:T(8,128)(2,1)S(1)}, u32[]{:S(2)}, u32[]{:S(2)}) %collective-permute-start.1) | collective-permute-done | bytes 49184 | tf_op jit(solution)/shard_map/ppermute | solution.py:236
  23.1 0.5 %collective-permute-done.2.rest_2_ = bf16[96,256]{1,0:T(8,128)(2,1)S(1)} collective-permute-done((bf16[96,256]{1,0:T(8,128)(2,1)}, bf16[96,256]{1,0:T(8,128)(2,1)S(1)}, u32[]{:S(2)}, u32[]{:S(2)}) %collective-permute-start.2) | collective-permute-done | bytes 49184 | tf_op jit(solution)/shard_map/ppermute | solution.py:236
  23.6 0.1 add_hops.1.own_ref.rest_0_
  23.7 0.1 collective-permute-start.3
  23.8 1.6 %collective-permute-start.5 = (bf16[128,256]{1,0:T(8,128)(2,1)S(1)}, bf16[128,256]{1,0:T(8,128)(2,1)S(1)}, u32[]{:S(2)}, u32[]{:S(2)}) collective-permute-start(bf16[128,256]{1,0:T(8,128)(2,1)S(1)} %add_hops.1.own_ref.rest_0_), channel_id=1, source_target_pairs={{0,12},{4,8},{8,4},{12,0},{1,13},{5,9},{9,5},{13,1},{2,14},{6,10},... | collective-permute-start | bytes 196616 | tf_op jit(solution)/shard_map/ppermute | solution.py:49
  25.4 0.5 %collective-permute-start.4 = (bf16[128,256]{1,0:T(8,128)(2,1)S(1)}, bf16[128,256]{1,0:T(8,128)(2,1)S(1)}, u32[]{:S(2)}, u32[]{:S(2)}) collective-permute-start(bf16[128,256]{1,0:T(8,128)(2,1)S(1)} %add_hops.1.own_ref.rest_0_), channel_id=1, source_target_pairs={{0,8},{4,12},{8,0},{12,4},{1,9},{5,13},{9,1},{13,5},{2,10},{6,14},... | collective-permute-start | bytes 196616 | tf_op jit(solution)/shard_map/ppermute | solution.py:49
  25.9 0.0 collective-permute-done.3.rest_1_
  25.9 1.7 %correlate_first.1 = (f32[2,2,256,1024]{3,2,1,0:T(8,128)}, bf16[1024,128]{1,0:T(8,128)(2,1)S(1)}) custom-call(s32[1]{0:T(128)} %bitcast.me_ref, bf16[128,256]{1,0:T(8,128)(2,1)S(1)} %add_hops.1.own_ref.rest_0_, bf16[128,256]{1,0:T(8,128)(2,1)S(1)} %add_hops.1.own_ref.rest_0_, bf16[128,256]{1,0:T(8,128)(2,1)S(1)} %collective-permute-done.3.rest_1_), custom_call_target="tpu_custom_call" | custom-call | flops 134217728 | bytes 2097152 | tf_op jit(solution)/shard_map/correlate_first/pallas_call | solution.py:274
  27.6 0.2 collective-permute-done.5.rest_0_
  27.8 1.2 %correlate_rest.2.rest_1_ = f32[2,2,256,1024]{3,2,1,0:T(8,128)} custom-call(s32[1]{0:T(128)} %bitcast.me_ref, bf16[1024,128]{1,0:T(8,128)(2,1)S(1)} %get-tuple-element.15.left_ref, bf16[128,256]{1,0:T(8,128)(2,1)S(1)} %collective-permute-done.5.rest_0_, f32[2,2,256,1024]{3,2,1,0:T(8,128)} %get-tuple-element.16.rest_1_), custom_call_target="tpu_custom_call", output_to_operand_aliasing={{}: (3, {})} | custom-call | tf_op jit(solution)/shard_map/correlate_rest/pallas_call | solution.py:285
  29.0 0.6 %collective-permute-done.4.rest_0_ = bf16[128,256]{1,0:T(8,128)(2,1)S(1)} collective-permute-done((bf16[128,256]{1,0:T(8,128)(2,1)S(1)}, bf16[128,256]{1,0:T(8,128)(2,1)S(1)}, u32[]{:S(2)}, u32[]{:S(2)}) %collective-permute-start.4) | collective-permute-done | bytes 65568 | tf_op jit(solution)/shard_map/ppermute | solution.py:49
  29.7 1.2 %correlate_rest.3 = f32[2,2,256,1024]{3,2,1,0:T(8,128)} custom-call(s32[1]{0:T(128)} %bitcast.me_ref, bf16[1024,128]{1,0:T(8,128)(2,1)S(1)} %get-tuple-element.15.left_ref, bf16[128,256]{1,0:T(8,128)(2,1)S(1)} %collective-permute-done.4.rest_0_, f32[2,2,256,1024]{3,2,1,0:T(8,128)} %correlate_rest.2.rest_1_), custom_call_target="tpu_custom_call", output_to_operand_aliasing={{}: (3, {})} | custom-call | tf_op jit(solution)/shard_map/correlate_rest/pallas_call | solution.py:285
Async XLA Ops:
  13.7 7.4 %collective-permute-start = (bf16[96,256]{1,0:T(8,128)(2,1)}, bf16[96,256]{1,0:T(8,128)(2,1)S(1)}, u32[]{:S(2)}, u32[]{:S(2)}) collective-permute-start(bf16[96,256]{1,0:T(8,128)(2,1)} %get-tuple-element.11), channel_id=1, source_target_pairs={{0,2},{1,3},{2,1},{3,0},{4,6},{5,7},{6,5},{7,4},{8,10},{9,11},{10,... | collective-permute-start | bytes 147464 | tf_op jit(solution)/shard_map/ppermute | solution.py:236
  17.8 5.4 %collective-permute-start.1 = (bf16[96,256]{1,0:T(8,128)(2,1)}, bf16[96,256]{1,0:T(8,128)(2,1)S(1)}, u32[]{:S(2)}, u32[]{:S(2)}) collective-permute-start(bf16[96,256]{1,0:T(8,128)(2,1)} %get-tuple-element.12), channel_id=1, source_target_pairs={{0,3},{1,2},{2,0},{3,1},{4,7},{5,6},{6,4},{7,5},{8,11},{9,10},{10,... | collective-permute-start | bytes 147464 | tf_op jit(solution)/shard_map/ppermute | solution.py:236
  18.9 4.7 %collective-permute-start.2 = (bf16[96,256]{1,0:T(8,128)(2,1)}, bf16[96,256]{1,0:T(8,128)(2,1)S(1)}, u32[]{:S(2)}, u32[]{:S(2)}) collective-permute-start(bf16[96,256]{1,0:T(8,128)(2,1)} %get-tuple-element.13), channel_id=1, source_target_pairs={{0,1},{1,0},{2,3},{3,2},{4,5},{5,4},{6,7},{7,6},{8,9},{9,8},{10,11... | collective-permute-start | bytes 147464 | tf_op jit(solution)/shard_map/ppermute | solution.py:236
  23.7 2.2 %collective-permute-start.3 = (bf16[128,256]{1,0:T(8,128)(2,1)S(1)}, bf16[128,256]{1,0:T(8,128)(2,1)S(1)}, u32[]{:S(2)}, u32[]{:S(2)}) collective-permute-start(bf16[128,256]{1,0:T(8,128)(2,1)S(1)} %add_hops.1.own_ref.rest_0_), channel_id=1, source_target_pairs={{0,4},{4,0},{8,12},{12,8},{1,5},{5,1},{9,13},{13,9},{2,6},{6,2},{1... | collective-permute-start | bytes 196616 | tf_op jit(solution)/shard_map/ppermute | solution.py:49
  23.8 4.1 %collective-permute-start.5 = (bf16[128,256]{1,0:T(8,128)(2,1)S(1)}, bf16[128,256]{1,0:T(8,128)(2,1)S(1)}, u32[]{:S(2)}, u32[]{:S(2)}) collective-permute-start(bf16[128,256]{1,0:T(8,128)(2,1)S(1)} %add_hops.1.own_ref.rest_0_), channel_id=1, source_target_pairs={{0,12},{4,8},{8,4},{12,0},{1,13},{5,9},{9,5},{13,1},{2,14},{6,10},... | collective-permute-start | bytes 196616 | tf_op jit(solution)/shard_map/ppermute | solution.py:49
  25.4 4.3 %collective-permute-start.4 = (bf16[128,256]{1,0:T(8,128)(2,1)S(1)}, bf16[128,256]{1,0:T(8,128)(2,1)S(1)}, u32[]{:S(2)}, u32[]{:S(2)}) collective-permute-start(bf16[128,256]{1,0:T(8,128)(2,1)S(1)} %add_hops.1.own_ref.rest_0_), channel_id=1, source_target_pairs={{0,8},{4,12},{8,0},{12,4},{1,9},{5,13},{9,1},{13,5},{2,10},{6,14},... | collective-permute-start | bytes 196616 | tf_op jit(solution)/shard_map/ppermute | solution.py:49

commit v4 on v3

--- a/solution.py
+++ b/solution.py
@@ -281,7 +281,7 @@
         compiler_params=pltpu.CompilerParams(vmem_limit_bytes=16 * MIB),
         name="correlate_first",
     )(my_block, spectra, spectra, *[arrived[slot] for slot in early])
-    for slot in reversed(late):
+    for slot in late:
         visibilities = pl.pallas_call(
             functools.partial(correlate_rest, scale, blocks, [slot]),
             in_specs=[smem, vmem, vmem, hbm],

time: 31 us -> 30.9 us (level)
  transfers between devices with their start and end apart: 6 -> 6, of which waited for: 5 -> 4; matrix products, arithmetic and copies ran while one was open for 3% -> 3% of each run, Pallas kernels for 9% -> 9%
where the time goes in v4:
time: 30.9 us; the launch traced here: 30.7 us
  Pallas kernels  17.9 us (58%)
  starting transfers between devices  7.61 us (25%)
  waiting for transfers between devices  4.28 us (14%)
  other arithmetic  0.9 us (3%)
    pallas_call x1, Pallas kernels, shards(): pl.pallas_call(functools.partial(channelize, slabs), in_specs=[pl.BlockSp...  13.7 us
    ppermute x3, starting transfers between devices, shards(): lax.ppermute(sent[slot], 'tm', list(enumerate(routes(slabs)[slot])))  5.68 us
    ppermute x3, waiting for transfers between devices, shards(): lax.ppermute(sent[slot], 'tm', list(enumerate(routes(slabs)[slot])))  3.33 us
    pallas_call x2, Pallas kernels, shards(): pl.pallas_call(functools.partial(correlate_rest, scale, blocks, [slot]),...  2.42 us
    ppermute x3, starting transfers between devices, exchange(): lax.ppermute(value, axis, [(source, partner(source, distance, count)) for...  1.93 us
    pallas_call x1, Pallas kernels, shards(): pl.pallas_call(functools.partial(correlate_first, scale, blocks, [0] + ea...  1.69 us
    ppermute x3, waiting for transfers between devices, exchange(): lax.ppermute(value, axis, [(source, partner(source, distance, count)) for...  0.95 us
    max x1, other arithmetic, shards(): jnp.maximum(sent[0], -FLAGGED)  0.9 us
  transfers between devices with their start and end apart: 6, of which 4 were waited for; matrix products, arithmetic and copies ran while one was open for 3% of the time, Pallas kernels for 9%

profile of v4, /device:TPU:0, one launch (start us, length us, event | category | flops | bytes accessed | tf_op | source)
XLA Modules:
  0.0 30.7 jit_solution(1575768772845754331)
XLA Ops:
  0.0 13.7 %channelize.1 = (f32[96,256]{1,0:T(8,128)}, bf16[96,256]{1,0:T(8,128)(2,1)}, bf16[96,256]{1,0:T(8,128)(2,1)}, bf16[96,256]{1,0:T(8,128)(2,1)}) custom-call(s32[1]{0:T(128)} %bitcast.1.me_ref, bf16[8,256,8192]{2,1,0:T(8,128)(2,1)} %samples_hbm.1, f32[16,8192]{1,0:T(8,128)} %fir_hbm.1, bf16[4,8,8192]{2,1,0:T(8,128)(2,1)} %constant.11.clone.table_hbm, ...), custom_call_target="tpu_custom_call" | custom-call | tf_op jit(solution)/shard_map/channelize/pallas_call | solution.py:213
  13.7 4.1 %collective-permute-start = (bf16[96,256]{1,0:T(8,128)(2,1)}, bf16[96,256]{1,0:T(8,128)(2,1)S(1)}, u32[]{:S(2)}, u32[]{:S(2)}) collective-permute-start(bf16[96,256]{1,0:T(8,128)(2,1)} %get-tuple-element.11), channel_id=1, source_target_pairs={{0,2},{1,3},{2,1},{3,0},{4,6},{5,7},{6,5},{7,4},{8,10},{9,11},{10,... | collective-permute-start | bytes 147464 | tf_op jit(solution)/shard_map/ppermute | solution.py:236
  17.8 1.1 %collective-permute-start.1 = (bf16[96,256]{1,0:T(8,128)(2,1)}, bf16[96,256]{1,0:T(8,128)(2,1)S(1)}, u32[]{:S(2)}, u32[]{:S(2)}) collective-permute-start(bf16[96,256]{1,0:T(8,128)(2,1)} %get-tuple-element.12), channel_id=1, source_target_pairs={{0,3},{1,2},{2,0},{3,1},{4,7},{5,6},{6,4},{7,5},{8,11},{9,10},{10,... | collective-permute-start | bytes 147464 | tf_op jit(solution)/shard_map/ppermute | solution.py:236
  18.9 0.5 %collective-permute-start.2 = (bf16[96,256]{1,0:T(8,128)(2,1)}, bf16[96,256]{1,0:T(8,128)(2,1)S(1)}, u32[]{:S(2)}, u32[]{:S(2)}) collective-permute-start(bf16[96,256]{1,0:T(8,128)(2,1)} %get-tuple-element.13), channel_id=1, source_target_pairs={{0,1},{1,0},{2,3},{3,2},{4,5},{5,4},{6,7},{7,6},{8,9},{9,8},{10,11... | collective-permute-start | bytes 147464 | tf_op jit(solution)/shard_map/ppermute | solution.py:236
  19.4 0.9 %broadcast_maximum_fusion.rest_3_ = f32[96,256]{1,0:T(8,128)S(1)} fusion(f32[96,256]{1,0:T(8,128)} %get-tuple-element.14), kind=kLoop, calls=%fused_computation | loop fusion | flops 24576 | bytes 196608 | tf_op jit(solution)/shard_map/max | solution.py:238
  20.3 0.9 %collective-permute-done.rest_0_ = bf16[96,256]{1,0:T(8,128)(2,1)S(1)} collective-permute-done((bf16[96,256]{1,0:T(8,128)(2,1)}, bf16[96,256]{1,0:T(8,128)(2,1)S(1)}, u32[]{:S(2)}, u32[]{:S(2)}) %collective-permute-start) | collective-permute-done | bytes 49184 | tf_op jit(solution)/shard_map/ppermute | solution.py:236
  21.1 2.0 %collective-permute-done.1.rest_1_ = bf16[96,256]{1,0:T(8,128)(2,1)S(1)} collective-permute-done((bf16[96,256]{1,0:T(8,128)(2,1)}, bf16[96,256]{1,0:T(8,128)(2,1)S(1)}, u32[]{:S(2)}, u32[]{:S(2)}) %collective-permute-start.1) | collective-permute-done | bytes 49184 | tf_op jit(solution)/shard_map/ppermute | solution.py:236
  23.1 0.5 %collective-permute-done.2.rest_2_ = bf16[96,256]{1,0:T(8,128)(2,1)S(1)} collective-permute-done((bf16[96,256]{1,0:T(8,128)(2,1)}, bf16[96,256]{1,0:T(8,128)(2,1)S(1)}, u32[]{:S(2)}, u32[]{:S(2)}) %collective-permute-start.2) | collective-permute-done | bytes 49184 | tf_op jit(solution)/shard_map/ppermute | solution.py:236
  23.6 0.1 add_hops.1.own_ref.rest_0_
  23.7 0.1 collective-permute-start.3
  23.8 1.6 %collective-permute-start.5 = (bf16[128,256]{1,0:T(8,128)(2,1)S(1)}, bf16[128,256]{1,0:T(8,128)(2,1)S(1)}, u32[]{:S(2)}, u32[]{:S(2)}) collective-permute-start(bf16[128,256]{1,0:T(8,128)(2,1)S(1)} %add_hops.1.own_ref.rest_0_), channel_id=1, source_target_pairs={{0,8},{4,12},{8,0},{12,4},{1,9},{5,13},{9,1},{13,5},{2,10},{6,14},... | collective-permute-start | bytes 196616 | tf_op jit(solution)/shard_map/ppermute | solution.py:49
  25.4 0.3 collective-permute-start.4
  25.6 0.0 collective-permute-done.3.rest_1_
  25.6 1.7 %correlate_first.1 = (f32[2,2,256,1024]{3,2,1,0:T(8,128)}, bf16[1024,128]{1,0:T(8,128)(2,1)S(1)}) custom-call(s32[1]{0:T(128)} %bitcast.me_ref, bf16[128,256]{1,0:T(8,128)(2,1)S(1)} %add_hops.1.own_ref.rest_0_, bf16[128,256]{1,0:T(8,128)(2,1)S(1)} %add_hops.1.own_ref.rest_0_, bf16[128,256]{1,0:T(8,128)(2,1)S(1)} %collective-permute-done.3.rest_1_), custom_call_target="tpu_custom_call" | custom-call | flops 134217728 | bytes 2097152 | tf_op jit(solution)/shard_map/correlate_first/pallas_call | solution.py:274
  27.3 0.9 %collective-permute-done.5.rest_0_ = bf16[128,256]{1,0:T(8,128)(2,1)S(1)} collective-permute-done((bf16[128,256]{1,0:T(8,128)(2,1)S(1)}, bf16[128,256]{1,0:T(8,128)(2,1)S(1)}, u32[]{:S(2)}, u32[]{:S(2)}) %collective-permute-start.5) | collective-permute-done | bytes 65568 | tf_op jit(solution)/shard_map/ppermute | solution.py:49
  28.3 1.2 %correlate_rest.2.rest_1_ = f32[2,2,256,1024]{3,2,1,0:T(8,128)} custom-call(s32[1]{0:T(128)} %bitcast.me_ref, bf16[1024,128]{1,0:T(8,128)(2,1)S(1)} %get-tuple-element.15.left_ref, bf16[128,256]{1,0:T(8,128)(2,1)S(1)} %collective-permute-done.5.rest_0_, f32[2,2,256,1024]{3,2,1,0:T(8,128)} %get-tuple-element.16.rest_1_), custom_call_target="tpu_custom_call", output_to_operand_aliasing={{}: (3, {})} | custom-call | tf_op jit(solution)/shard_map/correlate_rest/pallas_call | solution.py:285
  29.5 0.0 collective-permute-done.4.rest_0_
  29.5 1.2 %correlate_rest.3 = f32[2,2,256,1024]{3,2,1,0:T(8,128)} custom-call(s32[1]{0:T(128)} %bitcast.me_ref, bf16[1024,128]{1,0:T(8,128)(2,1)S(1)} %get-tuple-element.15.left_ref, bf16[128,256]{1,0:T(8,128)(2,1)S(1)} %collective-permute-done.4.rest_0_, f32[2,2,256,1024]{3,2,1,0:T(8,128)} %correlate_rest.2.rest_1_), custom_call_target="tpu_custom_call", output_to_operand_aliasing={{}: (3, {})} | custom-call | tf_op jit(solution)/shard_map/correlate_rest/pallas_call | solution.py:285
Async XLA Ops:
  13.7 7.4 %collective-permute-start = (bf16[96,256]{1,0:T(8,128)(2,1)}, bf16[96,256]{1,0:T(8,128)(2,1)S(1)}, u32[]{:S(2)}, u32[]{:S(2)}) collective-permute-start(bf16[96,256]{1,0:T(8,128)(2,1)} %get-tuple-element.11), channel_id=1, source_target_pairs={{0,2},{1,3},{2,1},{3,0},{4,6},{5,7},{6,5},{7,4},{8,10},{9,11},{10,... | collective-permute-start | bytes 147464 | tf_op jit(solution)/shard_map/ppermute | solution.py:236
  17.8 5.4 %collective-permute-start.1 = (bf16[96,256]{1,0:T(8,128)(2,1)}, bf16[96,256]{1,0:T(8,128)(2,1)S(1)}, u32[]{:S(2)}, u32[]{:S(2)}) collective-permute-start(bf16[96,256]{1,0:T(8,128)(2,1)} %get-tuple-element.12), channel_id=1, source_target_pairs={{0,3},{1,2},{2,0},{3,1},{4,7},{5,6},{6,4},{7,5},{8,11},{9,10},{10,... | collective-permute-start | bytes 147464 | tf_op jit(solution)/shard_map/ppermute | solution.py:236
  18.9 4.7 %collective-permute-start.2 = (bf16[96,256]{1,0:T(8,128)(2,1)}, bf16[96,256]{1,0:T(8,128)(2,1)S(1)}, u32[]{:S(2)}, u32[]{:S(2)}) collective-permute-start(bf16[96,256]{1,0:T(8,128)(2,1)} %get-tuple-element.13), channel_id=1, source_target_pairs={{0,1},{1,0},{2,3},{3,2},{4,5},{5,4},{6,7},{7,6},{8,9},{9,8},{10,11... | collective-permute-start | bytes 147464 | tf_op jit(solution)/shard_map/ppermute | solution.py:236
  23.7 1.9 %collective-permute-start.3 = (bf16[128,256]{1,0:T(8,128)(2,1)S(1)}, bf16[128,256]{1,0:T(8,128)(2,1)S(1)}, u32[]{:S(2)}, u32[]{:S(2)}) collective-permute-start(bf16[128,256]{1,0:T(8,128)(2,1)S(1)} %add_hops.1.own_ref.rest_0_), channel_id=1, source_target_pairs={{0,4},{4,0},{8,12},{12,8},{1,5},{5,1},{9,13},{13,9},{2,6},{6,2},{1... | collective-permute-start | bytes 196616 | tf_op jit(solution)/shard_map/ppermute | solution.py:49
  23.8 4.5 %collective-permute-start.5 = (bf16[128,256]{1,0:T(8,128)(2,1)S(1)}, bf16[128,256]{1,0:T(8,128)(2,1)S(1)}, u32[]{:S(2)}, u32[]{:S(2)}) collective-permute-start(bf16[128,256]{1,0:T(8,128)(2,1)S(1)} %add_hops.1.own_ref.rest_0_), channel_id=1, source_target_pairs={{0,8},{4,12},{8,0},{12,4},{1,9},{5,13},{9,1},{13,5},{2,10},{6,14},... | collective-permute-start | bytes 196616 | tf_op jit(solution)/shard_map/ppermute | solution.py:49
  25.4 4.2 %collective-permute-start.4 = (bf16[128,256]{1,0:T(8,128)(2,1)S(1)}, bf16[128,256]{1,0:T(8,128)(2,1)S(1)}, u32[]{:S(2)}, u32[]{:S(2)}) collective-permute-start(bf16[128,256]{1,0:T(8,128)(2,1)S(1)} %add_hops.1.own_ref.rest_0_), channel_id=1, source_target_pairs={{0,12},{4,8},{8,4},{12,0},{1,13},{5,9},{9,5},{13,1},{2,14},{6,10},... | collective-permute-start | bytes 196616 | tf_op jit(solution)/shard_map/ppermute | solution.py:49
